TPU v7x, 32 devices: a whole 2x2x4 slice. The times are simulated.
32 devices in a mesh: tp: 2 (over y), cp: 16 (over z, x, core).
Axes of the slice: x: 2, y: 2, z: 4, core: 2. Of those that a mesh axis runs over, the one named last changes fastest.
Arguments:
- features: bfloat16 [3, 2176, 8192], P(None, 'cp', 'tp'), may hold values from -6 to 6
- short_filter: float32 [3, 3, 8192], P(None, None, 'tp'), may hold values from -4 to 4
- long_filter: float32 [128, 8192], P(None, 'tp'), may hold values from -0.5 to 0.5
- skip_scale: float32 [8192], P('tp'), may hold values from -4 to 4
- out_weight: bfloat16 [8192, 8192], P('tp', 'cp'), may hold values from -0.09375 to 0.09375
Outputs:
- mixed: bfloat16 [2176, 8192], P('cp', 'tp')
All inputs are finite; a program needn't handle non-finite values.
Results may differ from a plain program's by a relative error of at most 0.017.
Values may be sent and summed in bfloat16 or wider, within the bound.
A program may use at most 192 MiB of HBM per device.

v0:
```python
import jax
import jax.numpy as jnp
from jax import lax
from jax.sharding import PartitionSpec as P

TAPS = 128
SHORT = 3


def from_behind(block, axis, distance):
    devices = range(lax.axis_size(axis))
    route = [(i - distance, i) for i in devices if i - distance in devices]
    return lax.ppermute(block, axis, route)


def short_conv(extended, short_filter):
    out_rows = extended.shape[1] - (SHORT - 1)
    summed = jnp.zeros((extended.shape[0], out_rows, extended.shape[2]), jnp.float32)
    for lag in range(SHORT):
        begin = SHORT - 1 - lag
        summed = summed + short_filter[:, lag, None, :] * extended[:, begin : begin + out_rows, :]
    return summed


def long_conv(product_ext, long_filter, skip_scale):
    out_rows = product_ext.shape[0] - (TAPS - 1)
    summed = skip_scale[None, :] * product_ext[TAPS - 1 :]
    for lag in range(TAPS):
        begin = TAPS - 1 - lag
        summed = summed + long_filter[lag][None, :] * product_ext[begin : begin + out_rows]
    return summed


def local(features, short_filter, long_filter, skip_scale, out_weight):
    tok_rows = features.shape[1]
    tail_rows = TAPS + SHORT - 2
    earlier = from_behind(features[:, tok_rows - tail_rows :, :], "cp", 1)
    extended = jnp.concatenate((earlier, features), axis=1).astype(jnp.float32)
    shorted = short_conv(extended, short_filter)
    product_ext = shorted[1] * shorted[2]
    filtered = long_conv(product_ext, long_filter, skip_scale)
    gated = (shorted[0, TAPS - 1 :] * filtered).astype(jnp.bfloat16)
    partial_value = jnp.dot(
        gated,
        lax.all_gather(out_weight, "cp", axis=1, tiled=True),
        preferred_element_type=jnp.float32,
    )
    mixed = lax.psum_scatter(
        partial_value.astype(jnp.bfloat16), "tp", scatter_dimension=1, tiled=True
    )
    return mixed


def solution(mesh):
    return jax.shard_map(
        local,
        mesh=mesh,
        in_specs=(P(None, "cp", "tp"), P(None, None, "tp"), P(None, "tp"), P("tp"), P("tp", "cp")),
        out_specs=P("cp", "tp"),
        check_vma=False,
    )
```

profile of v0, /device:TPU:5, one launch (start us, length us, event | category | flops | bytes accessed | tf_op | source)
XLA Modules:
  0.0 432.5 jit_solution(9747119177244924758)
XLA Ops:
  6.5 0.0 all-gather.2.cloned.1.call-start
  6.5 0.7 all-gather.2.cloned.1.call-update
  7.3 0.0 copy-start.3
  7.3 0.0 reduce-scatter.2.cloned.1.call-start
  7.3 1.2 copy-done.1
  8.5 0.8 slice.1184
  9.3 0.0 copy-start.44
  9.3 3.7 collective-permute-start
  13.0 0.0 copy-done.3
  13.0 0.1 fusion.267
  13.1 0.0 copy-done.2
  13.1 0.2 fusion.266
  13.3 0.9 fusion.264
  14.2 0.9 fusion.263
  15.1 0.9 fusion.265
  16.1 0.1 copy_bitcast_fusion
  16.2 0.0 copy-done.44
  16.2 0.6 add.523
  16.8 0.9 fusion.262
  17.7 0.9 fusion.261
  18.6 0.9 fusion.260
  19.5 94.1 %collective-permute-done = bf16[3,129,4096]{2,1,0:T(8,128)(2,1)S(1)} collective-permute-done((bf16[3,129,4096]{2,1,0:T(8,128)(2,1)S(1)}, bf16[3,129,4096]{2,1,0:T(8,128)(2,1)S(1)}, u32[]{:S(2)}, u32[]{:S(2)}) %collective-permute-start) | collective-permute-done | bytes 3170336 | tf_op jit(solution)/shard_map/ppermute | solution.py:13
  113.6 6.8 %maximum_convert_fusion = f32[3,265,4096]{2,1,0:T(8,128)} fusion(bf16[3,136,4096]{2,1,0:T(8,128)(2,1)S(1)} %copy-done.1, bf16[3,129,4096]{2,1,0:T(8,128)(2,1)S(1)} %collective-permute-done), kind=kLoop, calls=%fused_computation.6 | loop fusion | flops 13025280 | bytes 19537920 | tf_op jit(solution)/shard_map/convert_element_type | solution.py:38
  120.4 17.1 %fusion = f32[3,263,4096]{2,1,0:T(8,128)S(1)} fusion(f32[3,265,4096]{2,1,0:T(8,128)} %maximum_convert_fusion, f32[3,4096]{1,0:T(4,128)S(1)} %get-tuple-element.136, f32[3,4096]{1,0:T(4,128)S(1)} %get-tuple-element.137, f32[3,4096]{1,0:T(4,128)S(1)} %bitcast.1682), kind=kLoop, calls=%fused_computation.1 | loop fusion | flops 16158720 | bytes 51855360 | tf_op jit(solution)/shard_map/add | solution.py:21
  137.5 0.0 copy-start
  137.5 0.0 copy-start.4
  137.5 0.0 copy-start.5
  137.5 0.0 copy-start.6
  137.6 0.0 copy-start.7
  137.6 0.0 copy-start.8
  137.6 0.0 copy-start.9
  137.6 0.0 copy-start.10
  137.6 0.0 copy-start.11
  137.6 0.0 copy-start.12
  137.6 0.0 copy-start.13
  137.6 0.0 copy-start.14
  137.6 0.0 copy-start.15
  137.6 0.0 copy-start.16
  137.7 0.0 copy-start.17
  137.7 0.0 copy-start.18
  137.9 2.5 slice_multiply_fusion.3
  140.5 3.4 copy-done
  143.9 0.0 copy-done.7
  144.2 169.1 %fusion.272 = bf16[136,4096]{1,0:T(8,128)(2,1)S(1)} fusion(f32[1,263,4096]{2,1,0:T(8,128)} %slice_multiply_fusion.3, f32[3,263,4096]{2,1,0:T(8,128)} %copy-done, f32[4096]{0:T(1024)} %add.523, f32[4096]{0:T(1024)S(1)} %bitcast.1694, f32[4096]{0:T(1024)S(1)} %bitcast.1695, f32[4096]{0:T(1024)} %bitcast.1792, f32[4096]{0:T(1024)} %bitcast.1793, ...), kind=kLoop, calls=%fused_computation.12.clone.clone.1 | loop fusion | flops 143163392 | bytes 290652160 | tf_op jit(solution)/shard_map/dot_general | solution.py:43
  313.3 50.7 %all-gather.2.cloned.1.call-done = bf16[4096,8192]{1,0:T(8,128)(2,1)} async-done(((bf16[4096,512]{1,0:T(8,128)(2,1)}), bf16[4096,8192]{1,0:T(8,128)(2,1)}) %all-gather.2.cloned.1.call-update) | async-done | bytes 67108880 | tf_op jit(solution)/shard_map/all_gather | solution.py:45
  364.0 24.5 %convolution_convert_fusion = bf16[136,8192]{1,0:T(8,128)(2,1)} fusion(bf16[4096,8192]{1,0:T(8,128)(2,1)} %all-gather.2.cloned.1.call-done, bf16[136,4096]{1,0:T(8,128)(2,1)S(1)} %fusion.272), kind=kOutput, calls=%fused_computation.5 | convolution fusion | flops 9127919616 | bytes 70451200 | tf_op jit(solution)/shard_map/dot_general | solution.py:43
  388.5 0.0 reduce-scatter.2.cloned.1.call-update
  388.5 37.2 %reduce-scatter.2.cloned.1.call-done = bf16[136,4096]{1,0:T(8,128)(2,1)} async-done(((bf16[136,8192]{1,0:T(8,128)(2,1)}), bf16[136,4096]{1,0:T(8,128)(2,1)}) %reduce-scatter.2.cloned.1.call-update) | async-done | bytes 1114128 | tf_op jit(solution)/shard_map/reduce_scatter | solution.py:48
  (67 shorter events, 0.2 us)
Async XLA Ops:
  6.5 1.9 copy-start.1
  6.5 357.5 %all-gather.2.cloned.1.call-start = ((), (), s32[]{:S(2)}) async-start(), calls=%async_computation.1 | async-start | bytes 71303168 | tf_op jit(solution)/shard_map/all_gather | solution.py:45
  7.3 5.7 %copy-start.3 = (f32[3,3,4096]{2,1,0:T(4,128)S(1)}, f32[3,3,4096]{2,1,0:T(4,128)}, u32[]{:S(2)}) copy-start(f32[3,3,4096]{2,1,0:T(4,128)} %param.6) | copy-start | bytes 442372
  7.3 418.4 %reduce-scatter.2.cloned.1.call-start = ((), (), s32[]{:S(2)}) async-start(), calls=%async_computation.2 | async-start | bytes 3342336 | tf_op jit(solution)/shard_map/reduce_scatter | solution.py:48
  8.5 4.6 %copy-start.2 = (f32[128,4096]{1,0:T(8,128)S(1)}, f32[128,4096]{1,0:T(8,128)}, u32[]{:S(2)}) copy-start(f32[128,4096]{1,0:T(8,128)} %param.7) | copy-start | bytes 6291460
  9.3 6.9 %copy-start.44 = (f32[4096]{0:T(1024)S(1)}, f32[4096]{0:T(1024)}, u32[]{:S(2)}) copy-start(f32[4096]{0:T(1024)} %param.8) | copy-start | bytes 49156
  9.3 104.3 %collective-permute-start = (bf16[3,129,4096]{2,1,0:T(8,128)(2,1)S(1)}, bf16[3,129,4096]{2,1,0:T(8,128)(2,1)S(1)}, u32[]{:S(2)}, u32[]{:S(2)}) collective-permute-start(bf16[3,129,4096]{2,1,0:T(8,128)(2,1)S(1)} %slice.1184), channel_id=1, source_target_pairs={{0,1},{1,2},{2,3},{3,4},{4,5},{5,6},{6,7},{7,8},{8,9},{9,10},{10,1... | collective-permute-start | bytes 9510920 | tf_op jit(solution)/shard_map/ppermute | solution.py:13
  137.5 6.3 %copy-start = (f32[3,263,4096]{2,1,0:T(8,128)}, f32[3,263,4096]{2,1,0:T(8,128)S(1)}, u32[]{:S(2)}) copy-start(f32[3,263,4096]{2,1,0:T(8,128)S(1)} %fusion) | copy-start | bytes 38780932
  137.5 6.3 %copy-start.4 = (f32[1,4096]{1,0:T(1,128)S(1)}, f32[1,4096]{1,0:T(1,128)}, u32[]{:S(2)}) copy-start(f32[1,4096]{1,0:T(1,128)} %get-tuple-element.81) | copy-start | bytes 49156
  137.5 6.3 %copy-start.5 = (f32[1,4096]{1,0:T(1,128)S(1)}, f32[1,4096]{1,0:T(1,128)}, u32[]{:S(2)}) copy-start(f32[1,4096]{1,0:T(1,128)} %get-tuple-element.82) | copy-start | bytes 49156
  137.5 6.3 %copy-start.6 = (f32[1,4096]{1,0:T(1,128)S(1)}, f32[1,4096]{1,0:T(1,128)}, u32[]{:S(2)}) copy-start(f32[1,4096]{1,0:T(1,128)} %get-tuple-element.83) | copy-start | bytes 49156
  137.6 6.3 %copy-start.7 = (f32[1,4096]{1,0:T(1,128)S(1)}, f32[1,4096]{1,0:T(1,128)}, u32[]{:S(2)}) copy-start(f32[1,4096]{1,0:T(1,128)} %get-tuple-element.84) | copy-start | bytes 49156
  137.6 6.3 %copy-start.8 = (f32[1,4096]{1,0:T(1,128)S(1)}, f32[1,4096]{1,0:T(1,128)}, u32[]{:S(2)}) copy-start(f32[1,4096]{1,0:T(1,128)} %get-tuple-element.85) | copy-start | bytes 49156
  137.6 6.3 %copy-start.9 = (f32[1,4096]{1,0:T(1,128)S(1)}, f32[1,4096]{1,0:T(1,128)}, u32[]{:S(2)}) copy-start(f32[1,4096]{1,0:T(1,128)} %get-tuple-element.86) | copy-start | bytes 49156
  137.6 6.3 %copy-start.10 = (f32[1,4096]{1,0:T(1,128)S(1)}, f32[1,4096]{1,0:T(1,128)}, u32[]{:S(2)}) copy-start(f32[1,4096]{1,0:T(1,128)} %get-tuple-element.87) | copy-start | bytes 49156
  137.6 6.3 %copy-start.11 = (f32[1,4096]{1,0:T(1,128)S(1)}, f32[1,4096]{1,0:T(1,128)}, u32[]{:S(2)}) copy-start(f32[1,4096]{1,0:T(1,128)} %get-tuple-element.88) | copy-start | bytes 49156
  137.6 6.3 %copy-start.12 = (f32[1,4096]{1,0:T(1,128)S(1)}, f32[1,4096]{1,0:T(1,128)}, u32[]{:S(2)}) copy-start(f32[1,4096]{1,0:T(1,128)} %get-tuple-element.89) | copy-start | bytes 49156
  137.6 6.3 %copy-start.13 = (f32[1,4096]{1,0:T(1,128)S(1)}, f32[1,4096]{1,0:T(1,128)}, u32[]{:S(2)}) copy-start(f32[1,4096]{1,0:T(1,128)} %get-tuple-element.90) | copy-start | bytes 49156
  137.6 6.3 %copy-start.14 = (f32[1,4096]{1,0:T(1,128)S(1)}, f32[1,4096]{1,0:T(1,128)}, u32[]{:S(2)}) copy-start(f32[1,4096]{1,0:T(1,128)} %get-tuple-element.91) | copy-start | bytes 49156
  137.6 6.3 %copy-start.15 = (f32[1,4096]{1,0:T(1,128)S(1)}, f32[1,4096]{1,0:T(1,128)}, u32[]{:S(2)}) copy-start(f32[1,4096]{1,0:T(1,128)} %get-tuple-element.92) | copy-start | bytes 49156
  137.6 6.3 %copy-start.16 = (f32[1,4096]{1,0:T(1,128)S(1)}, f32[1,4096]{1,0:T(1,128)}, u32[]{:S(2)}) copy-start(f32[1,4096]{1,0:T(1,128)} %get-tuple-element.93) | copy-start | bytes 49156
  137.7 6.3 %copy-start.17 = (f32[1,4096]{1,0:T(1,128)S(1)}, f32[1,4096]{1,0:T(1,128)}, u32[]{:S(2)}) copy-start(f32[1,4096]{1,0:T(1,128)} %get-tuple-element.94) | copy-start | bytes 49156
  137.7 6.3 %copy-start.18 = (f32[1,4096]{1,0:T(1,128)S(1)}, f32[1,4096]{1,0:T(1,128)}, u32[]{:S(2)}) copy-start(f32[1,4096]{1,0:T(1,128)} %get-tuple-element.95) | copy-start | bytes 49156
  137.7 6.3 %copy-start.19 = (f32[1,4096]{1,0:T(1,128)S(1)}, f32[1,4096]{1,0:T(1,128)}, u32[]{:S(2)}) copy-start(f32[1,4096]{1,0:T(1,128)} %get-tuple-element.96) | copy-start | bytes 49156
  137.7 6.3 %copy-start.20 = (f32[1,4096]{1,0:T(1,128)S(1)}, f32[1,4096]{1,0:T(1,128)}, u32[]{:S(2)}) copy-start(f32[1,4096]{1,0:T(1,128)} %get-tuple-element.97) | copy-start | bytes 49156
  137.7 6.3 %copy-start.21 = (f32[1,4096]{1,0:T(1,128)S(1)}, f32[1,4096]{1,0:T(1,128)}, u32[]{:S(2)}) copy-start(f32[1,4096]{1,0:T(1,128)} %get-tuple-element.98) | copy-start | bytes 49156
  137.7 6.3 %copy-start.22 = (f32[1,4096]{1,0:T(1,128)S(1)}, f32[1,4096]{1,0:T(1,128)}, u32[]{:S(2)}) copy-start(f32[1,4096]{1,0:T(1,128)} %get-tuple-element.99) | copy-start | bytes 49156
  137.7 6.3 %copy-start.23 = (f32[1,4096]{1,0:T(1,128)S(1)}, f32[1,4096]{1,0:T(1,128)}, u32[]{:S(2)}) copy-start(f32[1,4096]{1,0:T(1,128)} %get-tuple-element.62) | copy-start | bytes 49156
  137.7 6.3 %copy-start.24 = (f32[1,4096]{1,0:T(1,128)S(1)}, f32[1,4096]{1,0:T(1,128)}, u32[]{:S(2)}) copy-start(f32[1,4096]{1,0:T(1,128)} %get-tuple-element.63) | copy-start | bytes 49156
  137.7 6.3 %copy-start.25 = (f32[1,4096]{1,0:T(1,128)S(1)}, f32[1,4096]{1,0:T(1,128)}, u32[]{:S(2)}) copy-start(f32[1,4096]{1,0:T(1,128)} %get-tuple-element.64) | copy-start | bytes 49156
  137.7 6.3 %copy-start.26 = (f32[1,4096]{1,0:T(1,128)S(1)}, f32[1,4096]{1,0:T(1,128)}, u32[]{:S(2)}) copy-start(f32[1,4096]{1,0:T(1,128)} %get-tuple-element.65) | copy-start | bytes 49156
  137.8 6.3 %copy-start.27 = (f32[1,4096]{1,0:T(1,128)S(1)}, f32[1,4096]{1,0:T(1,128)}, u32[]{:S(2)}) copy-start(f32[1,4096]{1,0:T(1,128)} %get-tuple-element.66) | copy-start | bytes 49156
  137.8 6.3 %copy-start.28 = (f32[1,4096]{1,0:T(1,128)S(1)}, f32[1,4096]{1,0:T(1,128)}, u32[]{:S(2)}) copy-start(f32[1,4096]{1,0:T(1,128)} %get-tuple-element.67) | copy-start | bytes 49156
  137.8 6.3 %copy-start.29 = (f32[1,4096]{1,0:T(1,128)S(1)}, f32[1,4096]{1,0:T(1,128)}, u32[]{:S(2)}) copy-start(f32[1,4096]{1,0:T(1,128)} %get-tuple-element.68) | copy-start | bytes 49156
  137.8 6.3 %copy-start.30 = (f32[1,4096]{1,0:T(1,128)S(1)}, f32[1,4096]{1,0:T(1,128)}, u32[]{:S(2)}) copy-start(f32[1,4096]{1,0:T(1,128)} %get-tuple-element.69) | copy-start | bytes 49156
  137.8 6.3 %copy-start.31 = (f32[1,4096]{1,0:T(1,128)S(1)}, f32[1,4096]{1,0:T(1,128)}, u32[]{:S(2)}) copy-start(f32[1,4096]{1,0:T(1,128)} %get-tuple-element.70) | copy-start | bytes 49156
  137.8 6.3 %copy-start.32 = (f32[1,4096]{1,0:T(1,128)S(1)}, f32[1,4096]{1,0:T(1,128)}, u32[]{:S(2)}) copy-start(f32[1,4096]{1,0:T(1,128)} %get-tuple-element.71) | copy-start | bytes 49156
  137.8 6.3 %copy-start.33 = (f32[1,4096]{1,0:T(1,128)S(1)}, f32[1,4096]{1,0:T(1,128)}, u32[]{:S(2)}) copy-start(f32[1,4096]{1,0:T(1,128)} %get-tuple-element.72) | copy-start | bytes 49156
  137.8 6.3 %copy-start.34 = (f32[1,4096]{1,0:T(1,128)S(1)}, f32[1,4096]{1,0:T(1,128)}, u32[]{:S(2)}) copy-start(f32[1,4096]{1,0:T(1,128)} %get-tuple-element.73) | copy-start | bytes 49156
  137.8 6.3 %copy-start.35 = (f32[1,4096]{1,0:T(1,128)S(1)}, f32[1,4096]{1,0:T(1,128)}, u32[]{:S(2)}) copy-start(f32[1,4096]{1,0:T(1,128)} %get-tuple-element.74) | copy-start | bytes 49156
  137.8 6.3 %copy-start.36 = (f32[1,4096]{1,0:T(1,128)S(1)}, f32[1,4096]{1,0:T(1,128)}, u32[]{:S(2)}) copy-start(f32[1,4096]{1,0:T(1,128)} %get-tuple-element.75) | copy-start | bytes 49156
  137.9 6.3 %copy-start.37 = (f32[1,4096]{1,0:T(1,128)S(1)}, f32[1,4096]{1,0:T(1,128)}, u32[]{:S(2)}) copy-start(f32[1,4096]{1,0:T(1,128)} %get-tuple-element.76) | copy-start | bytes 49156
  137.9 6.3 %copy-start.38 = (f32[1,4096]{1,0:T(1,128)S(1)}, f32[1,4096]{1,0:T(1,128)}, u32[]{:S(2)}) copy-start(f32[1,4096]{1,0:T(1,128)} %get-tuple-element.77) | copy-start | bytes 49156
  137.9 6.3 %copy-start.39 = (f32[1,4096]{1,0:T(1,128)S(1)}, f32[1,4096]{1,0:T(1,128)}, u32[]{:S(2)}) copy-start(f32[1,4096]{1,0:T(1,128)} %get-tuple-element.78) | copy-start | bytes 49156
  137.9 6.3 %copy-start.40 = (f32[1,4096]{1,0:T(1,128)S(1)}, f32[1,4096]{1,0:T(1,128)}, u32[]{:S(2)}) copy-start(f32[1,4096]{1,0:T(1,128)} %get-tuple-element.79) | copy-start | bytes 49156
  137.9 6.3 %copy-start.41 = (f32[1,4096]{1,0:T(1,128)S(1)}, f32[1,4096]{1,0:T(1,128)}, u32[]{:S(2)}) copy-start(f32[1,4096]{1,0:T(1,128)} %get-tuple-element.80) | copy-start | bytes 49156
  137.9 6.3 %copy-start.42 = (f32[1,4096]{1,0:T(1,128)S(1)}, f32[1,4096]{1,0:T(1,128)}, u32[]{:S(2)}) copy-start(f32[1,4096]{1,0:T(1,128)} %get-tuple-element.100) | copy-start | bytes 49156
  137.9 6.3 %copy-start.43 = (f32[1,4096]{1,0:T(1,128)S(1)}, f32[1,4096]{1,0:T(1,128)}, u32[]{:S(2)}) copy-start(f32[1,4096]{1,0:T(1,128)} %get-tuple-element.101) | copy-start | bytes 49156
Sparse Core Ops, SparseCore 0:
  8.9 355.0 all-gather.1
  388.7 36.9 reduce-scatter.1
where the time goes:
time: 435 us; the launch traced here: 433 us
  other arithmetic  196 us (45%)
  waiting for transfers between devices  183 us (42%)
  matrix products  24.5 us (6%)
  between operations  14.1 us (3%)
  local copies, waits for them, and re-layouts  11.4 us (3%)
    dot_general x1, other arithmetic, local(): jnp.dot(gated, lax.all_gather(out_weight, 'cp', axis=1, tiled=True), pref...  169 us
    ppermute x1, waiting for transfers between devices, from_behind(): return lax.ppermute(block, axis, route)  94.1 us
    all_gather x1, waiting for transfers between devices, local(): lax.all_gather(out_weight, 'cp', axis=1, tiled=True)  50.7 us
    reduce_scatter x1, waiting for transfers between devices, local(): lax.psum_scatter(partial_value.astype(jnp.bfloat16), 'tp', scatter_dimens...  37.2 us
    dot_general x1, matrix products, local(): jnp.dot(gated, lax.all_gather(out_weight, 'cp', axis=1, tiled=True), pref...  24.5 us
    add x1, other arithmetic, short_conv(): summed + short_filter[:, lag, None, :] * extended[:, begin:begin + out_ro...  17.1 us
  transfers between devices with their start and end apart: 3, of which 3 were waited for; matrix products, arithmetic and copies ran while one was open for 47% of the time, Pallas kernels for 0%

commit v1 on v0

v1 whole, which is shorter than its diff:
```python
import functools

import jax
import jax.numpy as jnp
from jax import lax
from jax.experimental import pallas as pl
from jax.experimental.pallas import tpu as pltpu
from jax.sharding import PartitionSpec as P

TAPS = 128
SHORT = 3
LANES = 128
SUB = 8


def from_behind(block, axis, distance):
    devices = range(lax.axis_size(axis))
    route = [(i - distance, i) for i in devices if i - distance in devices]
    return lax.ppermute(block, axis, route)


def conv_kernel(rows, width, feat_ref, halo_ref, edge_ref, short_ref, long_ref, skip_ref, out_ref, ext, prod):
    def strip(index, carry):
        lanes = pl.ds(pl.multiple_of(index * LANES, LANES), LANES)
        shorted = []
        for i in range(3):
            ext[i, pl.ds(0, SUB), :] = edge_ref[i, :, lanes].astype(jnp.float32)
            ext[i, pl.ds(SUB, rows), :] = feat_ref[i, :, lanes].astype(jnp.float32)
            total = short_ref[i, pl.ds(0, 1), lanes] * ext[i, pl.ds(SUB, rows), :]
            for lag in range(1, SHORT):
                total = total + short_ref[i, pl.ds(lag, 1), lanes] * ext[i, pl.ds(SUB - lag, rows), :]
            shorted.append(total)
        product = shorted[1] * shorted[2]
        prod[pl.ds(0, TAPS), :] = halo_ref[:, lanes].astype(jnp.float32)
        prod[pl.ds(TAPS, rows), :] = product
        total = skip_ref[:, lanes] * product
        span = rows + TAPS - SUB
        for r in range(SUB):
            shifted = prod[pl.ds(SUB - r, span), :]
            for m in range(TAPS // SUB):
                begin = TAPS - SUB - SUB * m
                total = total + long_ref[pl.ds(SUB * m + r, 1), lanes] * shifted[begin:begin + rows]
        out_ref[:, lanes] = (shorted[0] * total).astype(jnp.bfloat16)
        return carry

    lax.fori_loop(0, width // LANES, strip, 0)


def gate_conv(features, halo, edge, short_filter, long_filter, skip_scale):
    _, rows, channels = features.shape
    width = min(512, channels)
    return pl.pallas_call(
        functools.partial(conv_kernel, rows, width),
        grid=(channels // width,),
        out_shape=jax.ShapeDtypeStruct((rows, channels), jnp.bfloat16),
        in_specs=[
            pl.BlockSpec((3, rows, width), lambda c: (0, 0, c)),
            pl.BlockSpec((TAPS, width), lambda c: (0, c)),
            pl.BlockSpec((3, SUB, width), lambda c: (0, 0, c)),
            pl.BlockSpec((3, SHORT, width), lambda c: (0, 0, c)),
            pl.BlockSpec((TAPS, width), lambda c: (0, c)),
            pl.BlockSpec((1, width), lambda c: (0, c)),
        ],
        out_specs=pl.BlockSpec((rows, width), lambda c: (0, c)),
        scratch_shapes=[
            pltpu.VMEM((3, SUB + rows, LANES), jnp.float32),
            pltpu.VMEM((TAPS + rows, LANES), jnp.float32),
        ],
        compiler_params=pltpu.CompilerParams(vmem_limit_bytes=32 * 2**20),
        cost_estimate=pl.CostEstimate(
            flops=2 * TAPS * rows * channels, bytes_accessed=10 * rows * channels, transcendentals=0
        ),
        name="gate_conv",
    )(features, halo, edge, short_filter, long_filter, skip_scale.reshape(1, channels))


def halo_of(features, short_filter):
    rows = features.shape[1]
    tail = features[1:, rows - TAPS - SHORT + 1:, :].astype(jnp.float32)
    shorted = sum(
        short_filter[1:, lag, None, :] * tail[:, SHORT - 1 - lag:SHORT - 1 - lag + TAPS] for lag in range(SHORT)
    )
    product = (shorted[0] * shorted[1]).astype(jnp.bfloat16)
    return product, features[:, rows - SUB:, :]


def local(features, short_filter, long_filter, skip_scale, out_weight):
    product, edge = halo_of(features, short_filter)
    halo = from_behind(product, "cp", 1)
    edge = from_behind(edge, "cp", 1)
    gated = gate_conv(features, halo, edge, short_filter, long_filter, skip_scale)
    everyone = lax.all_gather(gated, "cp", axis=0, tiled=True)
    partial_value = jnp.dot(everyone, out_weight, preferred_element_type=jnp.float32).astype(jnp.bfloat16)
    mine = lax.all_to_all(partial_value, "cp", split_axis=0, concat_axis=1, tiled=True)
    return lax.psum_scatter(mine, "tp", scatter_dimension=1, tiled=True)


def solution(mesh):
    return jax.shard_map(
        local,
        mesh=mesh,
        in_specs=(P(None, "cp", "tp"), P(None, None, "tp"), P(None, "tp"), P("tp"), P("tp", "cp")),
        out_specs=P("cp", "tp"),
        check_vma=False,
    )
```

time: 435 us -> 261 us (0.60)
  other arithmetic: 196 us -> 3.68 us
  blocking collectives: 0 us -> 56.5 us
  waiting for transfers between devices: 183 us -> 139 us
  Pallas kernels: 0 us -> 22.7 us
  matrix products: 24.5 us -> 14.3 us
  local copies, waits for them, and re-layouts: 11.4 us -> 2.88 us
    dot_general x1 -> x0, other arithmetic: 169 us -> none  [local(): jnp.dot(gated, lax.all_gather(out_weight, 'cp', axis=1, tiled=True), pref...]
    ppermute x1 -> x2, waiting for transfers between devices: 94.1 us -> 11.9 us  [from_behind(): return lax.ppermute(block, axis, route)]
    all_to_all x0 -> x1, blocking collectives: none -> 56.5 us  [local(): lax.all_to_all(partial_value, 'cp', split_axis=0, concat_axis=1, tiled=True)]
    all_gather x1, waiting for transfers between devices: 50.7 us -> 96.5 us  [local(): everyone = lax.all_gather(gated, 'cp', axis=0, tiled=True)]
    pallas_call x0 -> x1, Pallas kernels: none -> 22.7 us  [gate_conv(): pl.pallas_call(functools.partial(conv_kernel, rows, width), grid=(channel...]
    add x1, other arithmetic: 17.1 us -> 1.22 us  [halo_of(): sum((short_filter[1:, lag, None, :] * tail[:, SHORT - 1 - lag:SHORT - 1 -...]
    dot_general x1, matrix products: 24.5 us -> 14.3 us  [local(): jnp.dot(everyone, out_weight, preferred_element_type=jnp.float32)]
    reduce_scatter x1, waiting for transfers between devices: 37.2 us -> 30.6 us  [local(): return lax.psum_scatter(mine, 'tp', scatter_dimension=1, tiled=True)]
  transfers between devices with their start and end apart: 3 -> 4, of which waited for: 3 -> 3; matrix products, arithmetic and copies ran while one was open for 47% -> 0% of each run, Pallas kernels for 0% -> 0%
where the time goes in v1:
time: 261 us; the launch traced here: 259 us
  waiting for transfers between devices  139 us (53%)
  blocking collectives  56.5 us (22%)
  Pallas kernels  22.7 us (9%)
  matrix products  14.3 us (5%)
  between operations  13.5 us (5%)
  starting transfers between devices  5.91 us (2%)
  other arithmetic  3.68 us (1%)
  local copies, waits for them, and re-layouts  2.88 us (1%)
    all_gather x1, waiting for transfers between devices, local(): everyone = lax.all_gather(gated, 'cp', axis=0, tiled=True)  96.5 us
    all_to_all x1, blocking collectives, local(): lax.all_to_all(partial_value, 'cp', split_axis=0, concat_axis=1, tiled=True)  56.5 us
    reduce_scatter x1, waiting for transfers between devices, local(): return lax.psum_scatter(mine, 'tp', scatter_dimension=1, tiled=True)  30.6 us
    pallas_call x1, Pallas kernels, gate_conv(): pl.pallas_call(functools.partial(conv_kernel, rows, width), grid=(channel...  22.7 us
    dot_general x1, matrix products, local(): jnp.dot(everyone, out_weight, preferred_element_type=jnp.float32)  14.3 us
    ppermute x2, waiting for transfers between devices, from_behind(): return lax.ppermute(block, axis, route)  11.9 us
    ppermute x2, starting transfers between devices, from_behind(): return lax.ppermute(block, axis, route)  5.86 us
  transfers between devices with their start and end apart: 4, of which 3 were waited for; matrix products, arithmetic and copies ran while one was open for 0% of the time, Pallas kernels for 0%

profile of v1, /device:TPU:5, one launch (start us, length us, event | category | flops | bytes accessed | tf_op | source)
XLA Modules:
  0.0 258.5 jit_solution(15429553192146514060)
XLA Ops:
  6.5 0.0 all-gather.2.cloned.1.call-start
  6.5 1.1 fusion.4
  7.7 2.2 slice_convert_fusion
  10.0 0.1 copy_bitcast_fusion
  10.0 0.0 copy-start.3
  10.0 1.2 fusion
  11.3 0.0 copy-start
  11.3 0.0 copy-start.1
  11.3 0.0 copy-start.2
  11.3 0.2 fusion.3
  11.5 3.9 %collective-permute-start = (bf16[128,4096]{1,0:T(8,128)(2,1)S(1)}, bf16[128,4096]{1,0:T(8,128)(2,1)S(1)}, u32[]{:S(2)}, u32[]{:S(2)}) collective-permute-start(bf16[128,4096]{1,0:T(8,128)(2,1)S(1)} %fusion.3), channel_id=1, source_target_pairs={{0,1},{1,2},{2,3},{3,4},{4,5},{5,6},{6,7},{7,8},{8,9},{9,10},{10,1... | collective-permute-start | bytes 3145736 | tf_op jit(solution)/shard_map/ppermute | solution.py:19
  15.5 0.0 copy-done
  15.5 1.9 collective-permute-start.1
  17.4 11.9 %collective-permute-done.1.edge_ref = bf16[3,8,4096]{2,1,0:T(8,128)(2,1)S(1)} collective-permute-done((bf16[3,8,4096]{2,1,0:T(8,128)(2,1)S(1)}, bf16[3,8,4096]{2,1,0:T(8,128)(2,1)S(1)}, u32[]{:S(2)}, u32[]{:S(2)}) %collective-permute-start.1) | collective-permute-done | bytes 196640 | tf_op jit(solution)/shard_map/ppermute | solution.py:19
  29.3 0.0 collective-permute-done.halo_ref
  29.3 0.0 copy-done.3
  29.3 0.0 copy-done.1
  29.3 0.0 copy-done.2
  29.3 22.7 %gate_conv.1 = bf16[136,4096]{1,0:T(8,128)(2,1)} custom-call(bf16[3,136,4096]{2,1,0:T(8,128)(2,1)S(1)} %copy-done, bf16[128,4096]{1,0:T(8,128)(2,1)S(1)} %collective-permute-done.halo_ref, bf16[3,8,4096]{2,1,0:T(8,128)(2,1)S(1)} %collective-permute-done.1.edge_ref, f32[3,3,4096]{2,1,0:T(4,128)S(1)} %copy-done.2, f32[128,4096]{1,0:T(8,128)S(1)} %copy-done.1, ...), custom_call_target="tpu_custom_call" | custom-call | flops 142606336 | bytes 5570560 | tf_op jit(solution)/shard_map/gate_conv/pallas_call | solution.py:52
  52.1 0.0 all-gather.2.cloned.1.call-update
  52.1 0.0 reduce-scatter.2.cloned.1.call-start
  52.1 96.5 %all-gather.2.cloned.1.call-done = bf16[2176,4096]{1,0:T(8,128)(2,1)} async-done(((bf16[136,4096]{1,0:T(8,128)(2,1)}), bf16[2176,4096]{1,0:T(8,128)(2,1)}) %all-gather.2.cloned.1.call-update) | async-done | bytes 17825808 | tf_op jit(solution)/shard_map/all_gather | solution.py:92
  148.6 14.3 %convolution_convert_fusion = bf16[2176,512]{1,0:T(8,128)(2,1)S(1)} fusion(bf16[2176,4096]{1,0:T(8,128)(2,1)} %all-gather.2.cloned.1.call-done, bf16[4096,512]{1,0:T(8,128)(2,1)} %param.9), kind=kOutput, calls=%fused_computation | convolution fusion | flops 9127919616 | bytes 24248320 | tf_op jit(solution)/shard_map/dot_general | solution.py:93
  162.9 56.5 %all_to_all.19 = bf16[16,136,512]{2,1,0:T(8,128)(2,1)S(1)} all-to-all(bf16[16,136,512]{2,1,0:T(8,128)(2,1)S(1)} %bitcast.19), channel_id=1, replica_groups=mesh['tp'=2,'cp'=16] {'cp'}, dimensions={0} | all-to-all | bytes 4456448 | tf_op jit(solution)/shard_map/all_to_all | solution.py:94
  219.4 1.6 copy.11
  221.0 0.0 reduce-scatter.2.cloned.1.call-update
  221.1 30.6 %reduce-scatter.2.cloned.1.call-done = bf16[136,4096]{1,0:T(8,128)(2,1)} async-done(((bf16[136,8192]{1,0:T(8,128)(2,1)}), bf16[136,4096]{1,0:T(8,128)(2,1)}) %reduce-scatter.2.cloned.1.call-update) | async-done | bytes 1114128 | tf_op jit(solution)/shard_map/reduce_scatter | solution.py:95
  (2 shorter events, 0.0 us)
Async XLA Ops:
  6.5 142.1 %all-gather.2.cloned.1.call-start = ((), (), s32[]{:S(2)}) async-start(), calls=%async_computation.2 | async-start | bytes 18939904 | tf_op jit(solution)/shard_map/all_gather | solution.py:92
  10.0 19.3 %copy-start.3 = (f32[4096]{0:T(1024)S(1)}, f32[4096]{0:T(1024)}, u32[]{:S(2)}) copy-start(f32[4096]{0:T(1024)} %param.8) | copy-start | bytes 49156
  11.3 4.2 %copy-start = (bf16[3,136,4096]{2,1,0:T(8,128)(2,1)S(1)}, bf16[3,136,4096]{2,1,0:T(8,128)(2,1)}, u32[]{:S(2)}) copy-start(bf16[3,136,4096]{2,1,0:T(8,128)(2,1)} %feat_ref.1) | copy-start | bytes 10027012
  11.3 18.0 %copy-start.1 = (f32[128,4096]{1,0:T(8,128)S(1)}, f32[128,4096]{1,0:T(8,128)}, u32[]{:S(2)}) copy-start(f32[128,4096]{1,0:T(8,128)} %long_ref.1) | copy-start | bytes 6291460
  11.3 18.0 %copy-start.2 = (f32[3,3,4096]{2,1,0:T(4,128)S(1)}, f32[3,3,4096]{2,1,0:T(4,128)}, u32[]{:S(2)}) copy-start(f32[3,3,4096]{2,1,0:T(4,128)} %short_ref.1) | copy-start | bytes 442372
  11.5 17.8 %collective-permute-start = (bf16[128,4096]{1,0:T(8,128)(2,1)S(1)}, bf16[128,4096]{1,0:T(8,128)(2,1)S(1)}, u32[]{:S(2)}, u32[]{:S(2)}) collective-permute-start(bf16[128,4096]{1,0:T(8,128)(2,1)S(1)} %fusion.3), channel_id=1, source_target_pairs={{0,1},{1,2},{2,3},{3,4},{4,5},{5,6},{6,7},{7,8},{8,9},{9,10},{10,1... | collective-permute-start | bytes 3145736 | tf_op jit(solution)/shard_map/ppermute | solution.py:19
  15.5 13.8 %collective-permute-start.1 = (bf16[3,8,4096]{2,1,0:T(8,128)(2,1)S(1)}, bf16[3,8,4096]{2,1,0:T(8,128)(2,1)S(1)}, u32[]{:S(2)}, u32[]{:S(2)}) collective-permute-start(bf16[3,8,4096]{2,1,0:T(8,128)(2,1)S(1)} %slice.39), channel_id=1, source_target_pairs={{0,1},{1,2},{2,3},{3,4},{4,5},{5,6},{6,7},{7,8},{8,9},{9,10},{10,1... | collective-permute-start | bytes 589832 | tf_op jit(solution)/shard_map/ppermute | solution.py:19
  52.1 199.6 %reduce-scatter.2.cloned.1.call-start = ((), (), s32[]{:S(2)}) async-start(), calls=%async_computation.3 | async-start | bytes 3342336 | tf_op jit(solution)/shard_map/reduce_scatter | solution.py:95
Sparse Core Ops, SparseCore 0:
  52.2 96.3 all-gather.1
  221.2 30.4 reduce-scatter.1

commit v2 on v1

--- a/solution.py
+++ b/solution.py
@@ -40,19 +40,23 @@
             for m in range(TAPS // SUB):
                 begin = TAPS - SUB - SUB * m
                 total = total + long_ref[pl.ds(SUB * m + r, 1), lanes] * shifted[begin:begin + rows]
-        out_ref[:, lanes] = (shorted[0] * total).astype(jnp.bfloat16)
+        out_ref[pl.ds(0, rows), lanes] = (shorted[0] * total).astype(jnp.bfloat16)
+        if out_ref.shape[0] > rows:
+            out_ref[pl.ds(rows, out_ref.shape[0] - rows), lanes] = jnp.zeros(
+                (out_ref.shape[0] - rows, LANES), jnp.bfloat16
+            )
         return carry
 
     lax.fori_loop(0, width // LANES, strip, 0)
 
 
-def gate_conv(features, halo, edge, short_filter, long_filter, skip_scale):
+def gate_conv(features, halo, edge, short_filter, long_filter, skip_scale, out_rows):
     _, rows, channels = features.shape
     width = min(512, channels)
     return pl.pallas_call(
         functools.partial(conv_kernel, rows, width),
         grid=(channels // width,),
-        out_shape=jax.ShapeDtypeStruct((rows, channels), jnp.bfloat16),
+        out_shape=jax.ShapeDtypeStruct((out_rows, channels), jnp.bfloat16),
         in_specs=[
             pl.BlockSpec((3, rows, width), lambda c: (0, 0, c)),
             pl.BlockSpec((TAPS, width), lambda c: (0, c)),
@@ -61,7 +65,7 @@
             pl.BlockSpec((TAPS, width), lambda c: (0, c)),
             pl.BlockSpec((1, width), lambda c: (0, c)),
         ],
-        out_specs=pl.BlockSpec((rows, width), lambda c: (0, c)),
+        out_specs=pl.BlockSpec((out_rows, width), lambda c: (0, c)),
         scratch_shapes=[
             pltpu.VMEM((3, SUB + rows, LANES), jnp.float32),
             pltpu.VMEM((TAPS + rows, LANES), jnp.float32),
@@ -84,11 +88,198 @@
     return product, features[:, rows - SUB:, :]
 
 
-def local(features, short_filter, long_filter, skip_scale, out_weight):
+def ring_kernel(
+    n, rows, gated_ref, weight_ref, out_ref, blocks, weights, kept, sent, other, summed, landed,
+    own_sem, block_send, block_recv, weight_send, weight_recv, tp_send, tp_recv, out_send, out_recv,
+):
+    t, cp = lax.axis_index("tp"), lax.axis_index("cp")
+    core, chip = cp % 2, cp // 2
+    x, z = chip % 2, chip // 2
+    depth = n // 2
+    place = x * (n - 1 - z) + (1 - x) * z
+    forth = 1 - 2 * core
+    half_owner = chip // depth
+    my_piece = (chip % depth) * 2 + t
+
+    def cp_at(ring_place):
+        r = (ring_place + 2 * n) % n
+        rx = r // depth
+        rz = rx * (n - 1 - r) + (1 - rx) * r
+        return (rz * 2 + rx) * 2 + core
+
+    def peer(a, b):
+        return dict(device_id=(a, b), device_id_type=pl.DeviceIdType.MESH)
+
+    ahead, behind = cp_at(place + forth), cp_at(place - forth)
+    sibling = cp + 1 - 2 * core
+
+    barrier = pltpu.get_barrier_semaphore()
+    for device in ((t, ahead), (t, behind), (t, sibling), (1 - t, cp)):
+        pl.semaphore_signal(barrier, inc=1, **peer(*device))
+
+    def greet(i, carry):
+        sender = (t * depth + i // 2) * 2 + core
+
+        @pl.when(jnp.logical_or(i % 2 != t, sender != cp))
+        def _():
+            pl.semaphore_signal(barrier, inc=1, **peer(i % 2, sender))
+
+        return carry
+
+    lax.fori_loop(0, n, greet, 0)
+    pl.semaphore_wait(barrier, 4 + n - 1 + (half_owner + t) % 2)
+
+    def send_own(slot, device):
+        return pltpu.make_async_remote_copy(
+            src_ref=gated_ref, dst_ref=blocks.at[slot], send_sem=block_send.at[slot], recv_sem=block_recv.at[slot],
+            **peer(t, device),
+        )
+
+    def pass_on(slot):
+        odd = slot % 2
+        return pltpu.make_async_remote_copy(
+            src_ref=blocks.at[slot], dst_ref=blocks.at[slot + 2], send_sem=block_send.at[slot + 2],
+            recv_sem=block_recv.at[slot + 2], **peer(t, odd * ahead + (1 - odd) * behind),
+        )
+
+    first, second = send_own(1, ahead), send_own(2, behind)
+    first.start()
+    second.start()
+    columns = pltpu.make_async_remote_copy(
+        src_ref=weight_ref, dst_ref=weights.at[core], send_sem=weight_send, recv_sem=weight_recv, **peer(t, sibling)
+    )
+    columns.start()
+    own_columns = pltpu.make_async_copy(weight_ref, weights.at[core], own_sem.at[0])
+    own_columns.start()
+    own_block = pltpu.make_async_copy(gated_ref, blocks.at[0], own_sem.at[1])
+    own_block.start()
+    own_columns.wait()
+    own_block.wait()
+    columns.wait_recv()
+
+    def tp_copy(slot):
+        return pltpu.make_async_remote_copy(
+            src_ref=sent.at[slot], dst_ref=other.at[slot], send_sem=tp_send.at[slot], recv_sem=tp_recv.at[slot],
+            **peer(1 - t, cp),
+        )
+
+    def out_copy(slot):
+        odd, step = slot % 2, (slot + 1) // 2
+        return pltpu.make_async_remote_copy(
+            src_ref=summed.at[slot], dst_ref=landed.at[my_piece], send_sem=out_send.at[slot],
+            recv_sem=out_recv.at[my_piece], **peer(half_owner, cp_at(place + (1 - 2 * odd) * forth * step)),
+        )
+
+    tile = min(256, weights.shape[2])
+
+    def multiply(slot, side, target):
+        def one(j, carry):
+            lanes = pl.ds(pl.multiple_of(j * tile, tile), tile)
+            target[slot, :, lanes] = jnp.dot(
+                blocks[slot], weights[side, :, lanes], preferred_element_type=jnp.float32
+            ).astype(jnp.bfloat16)
+            return carry
+
+        lax.fori_loop(0, weights.shape[2] // tile, one, 0)
+
+    def finish(slot):
+        tp_copy(slot).wait_recv()
+        total = (kept[slot].astype(jnp.float32) + other[slot].astype(jnp.float32)).astype(jnp.bfloat16)
+        stays = jnp.logical_and(slot == 0, half_owner == t)
+
+        @pl.when(stays)
+        def _():
+            landed[my_piece] = total
+
+        @pl.when(jnp.logical_not(stays))
+        def _():
+            summed[slot] = total
+            out_copy(slot).start()
+
+    def step(slot, carry):
+        @pl.when(slot > 0)
+        def _():
+            pltpu.make_async_copy(blocks.at[slot], blocks.at[slot], block_recv.at[slot]).wait()
+
+        @pl.when(jnp.logical_and(slot > 0, slot + 2 < n))
+        def _():
+            pass_on(slot).start()
+
+        multiply(slot, 1 - t, sent)
+        tp_copy(slot).start()
+        multiply(slot, t, kept)
+
+        @pl.when(slot > 0)
+        def _():
+            finish(slot - 1)
+
+        return carry
+
+    lax.fori_loop(0, n, step, 0)
+    finish(n - 1)
+
+    first.wait_send()
+    second.wait_send()
+    columns.wait_send()
+
+    def drain(slot, carry):
+        @pl.when(jnp.logical_and(slot > 0, slot + 2 < n))
+        def _():
+            pass_on(slot).wait_send()
+
+        tp_copy(slot).wait_send()
+
+        @pl.when(jnp.logical_not(jnp.logical_and(slot == 0, half_owner == t)))
+        def _():
+            out_copy(slot).wait_send()
+
+        return carry
+
+    lax.fori_loop(0, n, drain, 0)
+    for piece in range(n):
+        @pl.when(jnp.logical_not(jnp.logical_and(piece == my_piece, half_owner == t)))
+        def _():
+            pltpu.make_async_copy(landed.at[piece], landed.at[piece], out_recv.at[piece]).wait()
+
+        width = landed.shape[2]
+        out_ref[:, pl.ds(piece * width, width)] = landed[piece, pl.ds(0, rows), :]
+
+
+def project(gated, out_weight, rows, n):
+    padded, channels = gated.shape
+    width = out_weight.shape[1]
+    kind = jnp.bfloat16
+    dma = pltpu.SemaphoreType.DMA
+    return pl.pallas_call(
+        functools.partial(ring_kernel, n, rows),
+        out_shape=jax.ShapeDtypeStruct((rows, n * width), kind),
+        in_specs=[pl.BlockSpec(memory_space=pl.ANY)] * 2,
+        out_specs=pl.BlockSpec(memory_space=pltpu.VMEM),
+        scratch_shapes=[
+            pltpu.VMEM((n, padded, channels), kind),
+            pltpu.VMEM((2, channels, width), kind),
+            *[pltpu.VMEM((n, padded, width), kind)] * 5,
+            dma((2,)), dma((n,)), dma((n,)), dma, dma, dma((n,)), dma((n,)), dma((n,)), dma((n,)),
+        ],
+        compiler_params=pltpu.CompilerParams(
+            collective_id=0, has_side_effects=True, vmem_limit_bytes=48 * 2**20
+        ),
+        cost_estimate=pl.CostEstimate(
+            flops=4 * n * padded * channels * width, bytes_accessed=4 * channels * width, transcendentals=0
+        ),
+        name="ring_project",
+    )(gated, out_weight)
+
+
+def local(on_ring, features, short_filter, long_filter, skip_scale, out_weight):
+    rows = features.shape[1]
     product, edge = halo_of(features, short_filter)
     halo = from_behind(product, "cp", 1)
     edge = from_behind(edge, "cp", 1)
-    gated = gate_conv(features, halo, edge, short_filter, long_filter, skip_scale)
+    out_rows = -(-rows // 16) * 16 if on_ring else rows
+    gated = gate_conv(features, halo, edge, short_filter, long_filter, skip_scale, out_rows)
+    if on_ring:
+        return project(gated, out_weight, rows, lax.axis_size("cp") // 2)
     everyone = lax.all_gather(gated, "cp", axis=0, tiled=True)
     partial_value = jnp.dot(everyone, out_weight, preferred_element_type=jnp.float32).astype(jnp.bfloat16)
     mine = lax.all_to_all(partial_value, "cp", split_axis=0, concat_axis=1, tiled=True)
@@ -96,8 +287,9 @@
 
 
 def solution(mesh):
+    on_ring = mesh.shape["tp"] == 2 and mesh.shape["cp"] == 16
     return jax.shard_map(
-        local,
+        functools.partial(local, on_ring),
         mesh=mesh,
         in_specs=(P(None, "cp", "tp"), P(None, None, "tp"), P(None, "tp"), P("tp"), P("tp", "cp")),
         out_specs=P("cp", "tp"),

time: 261 us -> 172 us (0.66)
  the two profiles are of different devices: /device:TPU:5 before, /device:TPU:14 now
where the time goes in v2:
time: 172 us
  Pallas kernels  147 us (85%)
  waiting for transfers between devices  12.7 us (7%)
  starting transfers between devices  5.74 us (3%)
  other arithmetic  3.67 us (2%)
  local copies, waits for them, and re-layouts  2.26 us (1%)
    pallas_call x1, Pallas kernels, project(): pl.pallas_call(functools.partial(ring_kernel, n, rows), out_shape=jax.Sha...  125 us
    pallas_call x1, Pallas kernels, gate_conv(): pl.pallas_call(functools.partial(conv_kernel, rows, width), grid=(channel...  22.1 us
    ppermute x2, waiting for transfers between devices, from_behind(): return lax.ppermute(block, axis, route)  12.7 us
    ppermute x2, starting transfers between devices, from_behind(): return lax.ppermute(block, axis, route)  5.74 us
  transfers between devices with their start and end apart: 2, of which 1 were waited for; matrix products, arithmetic and copies ran while one was open for 0% of the time, Pallas kernels for 0%

profile of v2, /device:TPU:14, one launch (start us, length us, event | category | flops | bytes accessed | tf_op | source)
XLA Modules:
  0.0 171.9 jit_solution(17024387470747484216)
XLA Ops:
  0.0 1.1 fusion.4
  1.2 2.2 %slice_convert_fusion = f32[2,130,4096]{2,1,0:T(8,128)S(1)} fusion(bf16[3,136,4096]{2,1,0:T(8,128)(2,1)} %feat_ref.1), kind=kLoop, calls=%fused_computation.5 | loop fusion | flops 1064960 | bytes 6389760 | tf_op jit(solution)/shard_map/convert_element_type | solution.py:83
  3.4 0.1 copy_bitcast_fusion
  3.5 0.0 copy-start.3
  3.5 1.2 fusion
  4.7 0.0 copy-start
  4.7 0.0 copy-start.1
  4.8 0.0 copy-start.2
  4.8 0.2 fusion.3
  5.0 2.2 %collective-permute-start = (bf16[128,4096]{1,0:T(8,128)(2,1)S(1)}, bf16[128,4096]{1,0:T(8,128)(2,1)S(1)}, u32[]{:S(2)}, u32[]{:S(2)}) collective-permute-start(bf16[128,4096]{1,0:T(8,128)(2,1)S(1)} %fusion.3), channel_id=1, source_target_pairs={{0,1},{1,2},{2,3},{3,4},{4,5},{5,6},{6,7},{7,8},{8,9},{9,10},{10,1... | collective-permute-start | bytes 3145736 | tf_op jit(solution)/shard_map/ppermute | solution.py:19
  7.2 0.0 copy-done
  7.2 3.6 %collective-permute-start.1 = (bf16[3,8,4096]{2,1,0:T(8,128)(2,1)S(1)}, bf16[3,8,4096]{2,1,0:T(8,128)(2,1)S(1)}, u32[]{:S(2)}, u32[]{:S(2)}) collective-permute-start(bf16[3,8,4096]{2,1,0:T(8,128)(2,1)S(1)} %slice.39), channel_id=1, source_target_pairs={{0,1},{1,2},{2,3},{3,4},{4,5},{5,6},{6,7},{7,8},{8,9},{9,10},{10,1... | collective-permute-start | bytes 589832 | tf_op jit(solution)/shard_map/ppermute | solution.py:19
  10.8 12.7 %collective-permute-done.1.edge_ref = bf16[3,8,4096]{2,1,0:T(8,128)(2,1)S(1)} collective-permute-done((bf16[3,8,4096]{2,1,0:T(8,128)(2,1)S(1)}, bf16[3,8,4096]{2,1,0:T(8,128)(2,1)S(1)}, u32[]{:S(2)}, u32[]{:S(2)}) %collective-permute-start.1) | collective-permute-done | bytes 196640 | tf_op jit(solution)/shard_map/ppermute | solution.py:19
  23.5 0.0 collective-permute-done.halo_ref
  23.5 0.0 copy-done.3
  23.5 0.0 copy-done.1
  23.5 0.0 copy-done.2
  23.5 22.1 %gate_conv.1.gated_ref = bf16[144,4096]{1,0:T(8,128)(2,1)S(1)} custom-call(bf16[3,136,4096]{2,1,0:T(8,128)(2,1)S(1)} %copy-done, bf16[128,4096]{1,0:T(8,128)(2,1)S(1)} %collective-permute-done.halo_ref, bf16[3,8,4096]{2,1,0:T(8,128)(2,1)S(1)} %collective-permute-done.1.edge_ref, f32[3,3,4096]{2,1,0:T(4,128)S(1)} %copy-done.2, f32[128,4096]{1,0:T(8,128)S(1)} %copy-done.1, ...), custom_call_target="tpu_custom_call" | custom-call | flops 142606336 | bytes 5570560 | tf_op jit(solution)/shard_map/gate_conv/pallas_call | solution.py:56
  45.6 125.3 %ring_project.1 = bf16[136,4096]{1,0:T(8,128)(2,1)S(1)} custom-call(bf16[144,4096]{1,0:T(8,128)(2,1)S(1)} %gate_conv.1.gated_ref, bf16[4096,512]{1,0:T(8,128)(2,1)} %weight_ref.1), custom_call_target="tpu_custom_call" | custom-call | flops 9663676416 | bytes 8388608 | tf_op jit(solution)/shard_map/ring_project/pallas_call | solution.py:253
  170.9 1.0 copy.14
  (2 shorter events, 0.0 us)
Async XLA Ops:
  3.5 20.0 %copy-start.3 = (f32[4096]{0:T(1024)S(1)}, f32[4096]{0:T(1024)}, u32[]{:S(2)}) copy-start(f32[4096]{0:T(1024)} %param.8) | copy-start | bytes 49156
  4.7 2.4 %copy-start = (bf16[3,136,4096]{2,1,0:T(8,128)(2,1)S(1)}, bf16[3,136,4096]{2,1,0:T(8,128)(2,1)}, u32[]{:S(2)}) copy-start(bf16[3,136,4096]{2,1,0:T(8,128)(2,1)} %feat_ref.1) | copy-start | bytes 10027012
  4.7 18.7 %copy-start.1 = (f32[128,4096]{1,0:T(8,128)S(1)}, f32[128,4096]{1,0:T(8,128)}, u32[]{:S(2)}) copy-start(f32[128,4096]{1,0:T(8,128)} %long_ref.1) | copy-start | bytes 6291460
  4.8 18.7 %copy-start.2 = (f32[3,3,4096]{2,1,0:T(4,128)S(1)}, f32[3,3,4096]{2,1,0:T(4,128)}, u32[]{:S(2)}) copy-start(f32[3,3,4096]{2,1,0:T(4,128)} %short_ref.1) | copy-start | bytes 442372
  5.0 18.5 %collective-permute-start = (bf16[128,4096]{1,0:T(8,128)(2,1)S(1)}, bf16[128,4096]{1,0:T(8,128)(2,1)S(1)}, u32[]{:S(2)}, u32[]{:S(2)}) collective-permute-start(bf16[128,4096]{1,0:T(8,128)(2,1)S(1)} %fusion.3), channel_id=1, source_target_pairs={{0,1},{1,2},{2,3},{3,4},{4,5},{5,6},{6,7},{7,8},{8,9},{9,10},{10,1... | collective-permute-start | bytes 3145736 | tf_op jit(solution)/shard_map/ppermute | solution.py:19
  7.2 16.3 %collective-permute-start.1 = (bf16[3,8,4096]{2,1,0:T(8,128)(2,1)S(1)}, bf16[3,8,4096]{2,1,0:T(8,128)(2,1)S(1)}, u32[]{:S(2)}, u32[]{:S(2)}) collective-permute-start(bf16[3,8,4096]{2,1,0:T(8,128)(2,1)S(1)} %slice.39), channel_id=1, source_target_pairs={{0,1},{1,2},{2,3},{3,4},{4,5},{5,6},{6,7},{7,8},{8,9},{9,10},{10,1... | collective-permute-start | bytes 589832 | tf_op jit(solution)/shard_map/ppermute | solution.py:19

commit v3 on v2

--- a/solution.py
+++ b/solution.py
@@ -88,11 +88,15 @@
     return product, features[:, rows - SUB:, :]
 
 
-def ring_kernel(
-    n, rows, gated_ref, weight_ref, out_ref, blocks, weights, kept, sent, other, summed, landed,
-    own_sem, block_send, block_recv, weight_send, weight_recv, tp_send, tp_recv, out_send, out_recv,
+def mixer_kernel(
+    n, parts, feat_ref, short_ref, long_ref, skip_ref, weight_ref, out_ref,
+    blocks, weights, kept, sent, other, summed, landed, totals, direct, edge_out, edge_in, tail_out, tail_in, ext, prod,
+    own_sem, edge_sem, tail_send, tail_recv, block_send, block_recv, weight_send, weight_recv,
+    tp_send, tp_recv, out_send, out_recv,
 ):
     t, cp = lax.axis_index("tp"), lax.axis_index("cp")
+    rows = feat_ref.shape[1]
+    padded, part = blocks.shape[2:]
     core, chip = cp % 2, cp // 2
     x, z = chip % 2, chip // 2
     depth = n // 2
@@ -112,11 +116,16 @@
 
     ahead, behind = cp_at(place + forth), cp_at(place - forth)
     sibling = cp + 1 - 2 * core
+    is_first, is_last = cp == 0, cp == 2 * n - 1
 
     barrier = pltpu.get_barrier_semaphore()
     for device in ((t, ahead), (t, behind), (t, sibling), (1 - t, cp)):
         pl.semaphore_signal(barrier, inc=1, **peer(*device))
 
+    @pl.when(cp > 0)
+    def _():
+        pl.semaphore_signal(barrier, inc=1, **peer(t, cp - 1))
+
     def greet(i, carry):
         sender = (t * depth + i // 2) * 2 + core
 
@@ -127,34 +136,154 @@
         return carry
 
     lax.fori_loop(0, n, greet, 0)
-    pl.semaphore_wait(barrier, 4 + n - 1 + (half_owner + t) % 2)
-
-    def send_own(slot, device):
-        return pltpu.make_async_remote_copy(
-            src_ref=gated_ref, dst_ref=blocks.at[slot], send_sem=block_send.at[slot], recv_sem=block_recv.at[slot],
-            **peer(t, device),
-        )
-
-    def pass_on(slot):
-        odd = slot % 2
-        return pltpu.make_async_remote_copy(
-            src_ref=blocks.at[slot], dst_ref=blocks.at[slot + 2], send_sem=block_send.at[slot + 2],
-            recv_sem=block_recv.at[slot + 2], **peer(t, odd * ahead + (1 - odd) * behind),
-        )
-
-    first, second = send_own(1, ahead), send_own(2, behind)
-    first.start()
-    second.start()
+    pl.semaphore_wait(barrier, 4 + n - 1 + (half_owner + t) % 2 + (2 * n - 1 - cp + 2 * n - 2) // (2 * n - 1))
+
     columns = pltpu.make_async_remote_copy(
         src_ref=weight_ref, dst_ref=weights.at[core], send_sem=weight_send, recv_sem=weight_recv, **peer(t, sibling)
     )
+    own_columns = pltpu.make_async_copy(weight_ref, weights.at[core], own_sem)
+    edge_copy = pltpu.make_async_remote_copy(
+        src_ref=edge_out, dst_ref=edge_in, send_sem=edge_sem.at[0], recv_sem=edge_sem.at[1], **peer(t, cp + 1)
+    )
+
+    def tail_copy(p):
+        return pltpu.make_async_remote_copy(
+            src_ref=tail_out.at[p], dst_ref=tail_in.at[p], send_sem=tail_send.at[p], recv_sem=tail_recv.at[p],
+            **peer(t, cp + 1),
+        )
+
+    def strip_of(index):
+        return pl.ds(pl.multiple_of(index * LANES, LANES), LANES)
+
+    strips = part // LANES
+
+    def edges(index, carry):
+        lanes = strip_of(index)
+        q, k, v = (feat_ref[i, pl.ds(rows - SUB, SUB), lanes].astype(jnp.float32) for i in range(3))
+        row = lax.broadcasted_iota(jnp.int32, (SUB, LANES), 0)
+        kv = jnp.where(row >= SUB - 2, k, pltpu.roll(v, SUB - 2, 0))
+        edge_out[:, lanes] = jnp.concatenate((q, kv), axis=0).astype(jnp.bfloat16)
+        return carry
+
+    lax.fori_loop(0, parts * strips, edges, 0)
+
+    @pl.when(jnp.logical_not(is_last))
+    def _():
+        edge_copy.start()
+
+    own_columns.start()
+
+    def short(i, lanes, begin, count):
+        total = short_ref[i, pl.ds(0, 1), lanes] * ext[i, pl.ds(SUB + begin, count), :]
+        for lag in range(1, SHORT):
+            total = total + short_ref[i, pl.ds(lag, 1), lanes] * ext[i, pl.ds(SUB + begin - lag, count), :]
+        return total
+
+    def tails(p, carry):
+        def one(s, carry):
+            lanes = strip_of(p * strips + s)
+            for i in (1, 2):
+                ext[i, pl.ds(SUB, rows), :] = feat_ref[i, :, lanes].astype(jnp.float32)
+            product = short(1, lanes, rows - TAPS, TAPS) * short(2, lanes, rows - TAPS, TAPS)
+            tail_out[p, :, strip_of(s)] = product.astype(jnp.bfloat16)
+            return carry
+
+        lax.fori_loop(0, strips, one, 0)
+
+        @pl.when(jnp.logical_not(is_last))
+        def _():
+            tail_copy(p).start()
+
+        return carry
+
+    lax.fori_loop(0, parts, tails, 0)
     columns.start()
-    own_columns = pltpu.make_async_copy(weight_ref, weights.at[core], own_sem.at[0])
-    own_columns.start()
-    own_block = pltpu.make_async_copy(gated_ref, blocks.at[0], own_sem.at[1])
-    own_block.start()
+
+    @pl.when(is_first)
+    def _():
+        edge_in[...] = jnp.zeros_like(edge_in)
+        tail_in[...] = jnp.zeros_like(tail_in)
+
+    @pl.when(jnp.logical_not(is_first))
+    def _():
+        edge_copy.wait_recv()
+
+    def extend(lanes, which):
+        edge = edge_in[:, lanes].astype(jnp.float32)
+        q, kv = edge[:SUB], edge[SUB:]
+        ahead_rows = (q, kv, pltpu.roll(kv, 2, 0))
+        for i in which:
+            ext[i, pl.ds(0, SUB), :] = ahead_rows[i]
+            ext[i, pl.ds(SUB, rows), :] = feat_ref[i, :, lanes].astype(jnp.float32)
+
+    prod[pl.ds(0, SUB), :] = jnp.zeros((SUB, LANES), jnp.float32)
+
+    def own_rows(index, carry):
+        lanes = strip_of(index)
+        extend(lanes, (1, 2))
+        product = short(1, lanes, 0, rows) * short(2, lanes, 0, rows)
+        prod[pl.ds(SUB, rows), :] = product
+        total = skip_ref[:, lanes] * product
+        for r in range(SUB):
+            shifted = prod[pl.ds(SUB - r, rows), :]
+            for m in range(TAPS // SUB):
+                tap = long_ref[pl.ds(SUB * m + r, 1), lanes]
+                rest = total[SUB * m:] + tap * shifted[:rows - SUB * m]
+                total = jnp.concatenate((total[:SUB * m], rest), axis=0) if m else rest
+        direct[:, lanes] = total
+        return carry
+
+    lax.fori_loop(0, parts * strips, own_rows, 0)
+
+    def send_own(slot, p, device):
+        return pltpu.make_async_remote_copy(
+            src_ref=blocks.at[0, p], dst_ref=blocks.at[slot, p], send_sem=block_send.at[slot, p],
+            recv_sem=block_recv.at[slot, p], **peer(t, device),
+        )
+
+    def pass_on(slot, p):
+        odd = slot % 2
+        return pltpu.make_async_remote_copy(
+            src_ref=blocks.at[slot, p], dst_ref=blocks.at[slot + 2, p], send_sem=block_send.at[slot + 2, p],
+            recv_sem=block_recv.at[slot + 2, p], **peer(t, odd * ahead + (1 - odd) * behind),
+        )
+
+    prod[pl.ds(TAPS, SUB), :] = jnp.zeros((SUB, LANES), jnp.float32)
+
+    def gates(p, carry):
+        @pl.when(jnp.logical_not(is_first))
+        def _():
+            tail_copy(p).wait_recv()
+
+        def one(s, carry):
+            lanes = strip_of(p * strips + s)
+            prod[pl.ds(0, TAPS), :] = tail_in[p, :, strip_of(s)].astype(jnp.float32)
+            total = direct[pl.ds(0, TAPS), lanes]
+            for r in range(SUB):
+                shifted = prod[pl.ds(SUB - r, TAPS), :]
+                for m in range(TAPS // SUB):
+                    tap = long_ref[pl.ds(SUB * m + r, 1), lanes]
+                    count = SUB * (m + 1)
+                    head = total[:count] + tap * shifted[TAPS - count:]
+                    total = jnp.concatenate((head, total[count:]), axis=0) if count < TAPS else head
+            extend(lanes, (0,))
+            gate = short(0, lanes, 0, rows)
+            later = jnp.concatenate(
+                (gate[TAPS:] * direct[pl.ds(TAPS, rows - TAPS), lanes],
+                 jnp.zeros((padded - rows, LANES), jnp.float32)), axis=0,
+            )
+            blocks[0, p, pl.ds(0, TAPS), strip_of(s)] = (gate[:TAPS] * total).astype(jnp.bfloat16)
+            blocks[0, p, pl.ds(TAPS, padded - TAPS), strip_of(s)] = later.astype(jnp.bfloat16)
+            return carry
+
+        lax.fori_loop(0, strips, one, 0)
+        send_own(1, p, ahead).start()
+        send_own(2, p, behind).start()
+        return carry
+
+    lax.fori_loop(0, parts, gates, 0)
+
     own_columns.wait()
-    own_block.wait()
     columns.wait_recv()
 
     def tp_copy(slot):
@@ -170,17 +299,29 @@
             recv_sem=out_recv.at[my_piece], **peer(half_owner, cp_at(place + (1 - 2 * odd) * forth * step)),
         )
 
-    tile = min(256, weights.shape[2])
-
-    def multiply(slot, side, target):
+    width = weights.shape[2]
+    tile = min(256, width)
+
+    def multiply(slot, p, first):
+        depth_rows = pl.ds(pl.multiple_of(p * part, part), part)
+
         def one(j, carry):
             lanes = pl.ds(pl.multiple_of(j * tile, tile), tile)
-            target[slot, :, lanes] = jnp.dot(
-                blocks[slot], weights[side, :, lanes], preferred_element_type=jnp.float32
-            ).astype(jnp.bfloat16)
+            for side in range(2):
+                value = jnp.dot(
+                    blocks[slot, p], weights[side, depth_rows, lanes], preferred_element_type=jnp.float32
+                )
+                if not first:
+                    value = value + totals[slot % 2, side, :, lanes]
+                totals[slot % 2, side, :, lanes] = value
             return carry
 
-        lax.fori_loop(0, weights.shape[2] // tile, one, 0)
+        lax.fori_loop(0, width // tile, one, 0)
+
+    def emit(slot):
+        sent[slot] = totals[slot % 2, 1 - t].astype(jnp.bfloat16)
+        tp_copy(slot).start()
+        kept[slot] = totals[slot % 2, t].astype(jnp.bfloat16)
 
     def finish(slot):
         tp_copy(slot).wait_recv()
@@ -196,37 +337,65 @@
             summed[slot] = total
             out_copy(slot).start()
 
-    def step(slot, carry):
-        @pl.when(slot > 0)
-        def _():
-            pltpu.make_async_copy(blocks.at[slot], blocks.at[slot], block_recv.at[slot]).wait()
-
-        @pl.when(jnp.logical_and(slot > 0, slot + 2 < n))
-        def _():
-            pass_on(slot).start()
-
-        multiply(slot, 1 - t, sent)
-        tp_copy(slot).start()
-        multiply(slot, t, kept)
-
-        @pl.when(slot > 0)
-        def _():
-            finish(slot - 1)
-
-        return carry
-
-    lax.fori_loop(0, n, step, 0)
+    def take(slot, p, first):
+        pltpu.make_async_copy(blocks.at[slot, p], blocks.at[slot, p], block_recv.at[slot, p]).wait()
+
+        @pl.when(slot + 2 < n)
+        def _():
+            pass_on(slot, p).start()
+
+        multiply(slot, p, first)
+
+    multiply(0, 0, True)
+    lax.fori_loop(1, parts, lambda p, carry: (multiply(0, p, False), carry)[1], 0)
+    emit(0)
+
+    def pair(i, carry):
+        odd, even = 2 * i - 1, 2 * i
+
+        def both(p, first):
+            take(odd, p, first)
+            take(even, p, first)
+
+        both(0, True)
+        lax.fori_loop(1, parts, lambda p, carry: (both(p, False), carry)[1], 0)
+        emit(odd)
+        emit(even)
+        finish(odd - 1)
+
+        @pl.when(i > 1)
+        def _():
+            finish(odd - 2)
+
+        return carry
+
+    lax.fori_loop(1, depth, pair, 0)
+    take(n - 1, 0, True)
+    finish(n - 2)
+    finish(n - 3)
+    lax.fori_loop(1, parts, lambda p, carry: (take(n - 1, p, False), carry)[1], 0)
+    emit(n - 1)
     finish(n - 1)
 
-    first.wait_send()
-    second.wait_send()
     columns.wait_send()
 
+    @pl.when(jnp.logical_not(is_last))
+    def _():
+        edge_copy.wait_send()
+
+    def drain_parts(p, carry):
+        @pl.when(jnp.logical_not(is_last))
+        def _():
+            tail_copy(p).wait_send()
+
+        send_own(1, p, ahead).wait_send()
+        send_own(2, p, behind).wait_send()
+        lax.fori_loop(1, n - 2, lambda slot, carry: (pass_on(slot, p).wait_send(), carry)[1], 0)
+        return carry
+
+    lax.fori_loop(0, parts, drain_parts, 0)
+
     def drain(slot, carry):
-        @pl.when(jnp.logical_and(slot > 0, slot + 2 < n))
-        def _():
-            pass_on(slot).wait_send()
-
         tp_copy(slot).wait_send()
 
         @pl.when(jnp.logical_not(jnp.logical_and(slot == 0, half_owner == t)))
@@ -241,45 +410,54 @@
         def _():
             pltpu.make_async_copy(landed.at[piece], landed.at[piece], out_recv.at[piece]).wait()
 
-        width = landed.shape[2]
         out_ref[:, pl.ds(piece * width, width)] = landed[piece, pl.ds(0, rows), :]
 
 
-def project(gated, out_weight, rows, n):
-    padded, channels = gated.shape
+def mixer(features, short_filter, long_filter, skip_scale, out_weight, n):
+    _, rows, channels = features.shape
+    padded = -(-rows // 16) * 16
     width = out_weight.shape[1]
+    parts = 4
+    part = channels // parts
     kind = jnp.bfloat16
     dma = pltpu.SemaphoreType.DMA
+    whole = pl.BlockSpec(memory_space=pltpu.VMEM)
     return pl.pallas_call(
-        functools.partial(ring_kernel, n, rows),
+        functools.partial(mixer_kernel, n, parts),
         out_shape=jax.ShapeDtypeStruct((rows, n * width), kind),
-        in_specs=[pl.BlockSpec(memory_space=pl.ANY)] * 2,
-        out_specs=pl.BlockSpec(memory_space=pltpu.VMEM),
+        in_specs=[whole] * 4 + [pl.BlockSpec(memory_space=pl.ANY)],
+        out_specs=whole,
         scratch_shapes=[
-            pltpu.VMEM((n, padded, channels), kind),
+            pltpu.VMEM((n, parts, padded, part), kind),
             pltpu.VMEM((2, channels, width), kind),
             *[pltpu.VMEM((n, padded, width), kind)] * 5,
-            dma((2,)), dma((n,)), dma((n,)), dma, dma, dma((n,)), dma((n,)), dma((n,)), dma((n,)),
+            pltpu.VMEM((2, 2, padded, width), jnp.float32),
+            pltpu.VMEM((rows, channels), jnp.float32),
+            *[pltpu.VMEM((2 * SUB, channels), kind)] * 2,
+            *[pltpu.VMEM((parts, TAPS, part), kind)] * 2,
+            pltpu.VMEM((3, SUB + rows, LANES), jnp.float32),
+            pltpu.VMEM((TAPS + 2 * SUB, LANES), jnp.float32),
+            dma, dma((2,)), dma((parts,)), dma((parts,)), dma((n, parts)), dma((n, parts)), dma, dma,
+            dma((n,)), dma((n,)), dma((n,)), dma((n,)),
         ],
         compiler_params=pltpu.CompilerParams(
-            collective_id=0, has_side_effects=True, vmem_limit_bytes=48 * 2**20
+            collective_id=0, has_side_effects=True, vmem_limit_bytes=56 * 2**20
         ),
         cost_estimate=pl.CostEstimate(
             flops=4 * n * padded * channels * width, bytes_accessed=4 * channels * width, transcendentals=0
         ),
-        name="ring_project",
-    )(gated, out_weight)
+        name="mixer",
+    )(features, short_filter, long_filter, skip_scale.reshape(1, channels), out_weight)
 
 
 def local(on_ring, features, short_filter, long_filter, skip_scale, out_weight):
     rows = features.shape[1]
+    if on_ring:
+        return mixer(features, short_filter, long_filter, skip_scale, out_weight, lax.axis_size("cp") // 2)
     product, edge = halo_of(features, short_filter)
     halo = from_behind(product, "cp", 1)
     edge = from_behind(edge, "cp", 1)
-    out_rows = -(-rows // 16) * 16 if on_ring else rows
-    gated = gate_conv(features, halo, edge, short_filter, long_filter, skip_scale, out_rows)
-    if on_ring:
-        return project(gated, out_weight, rows, lax.axis_size("cp") // 2)
+    gated = gate_conv(features, halo, edge, short_filter, long_filter, skip_scale, rows)
     everyone = lax.all_gather(gated, "cp", axis=0, tiled=True)
     partial_value = jnp.dot(everyone, out_weight, preferred_element_type=jnp.float32).astype(jnp.bfloat16)
     mine = lax.all_to_all(partial_value, "cp", split_axis=0, concat_axis=1, tiled=True)

time: 172 us -> 144 us (0.84)
  the two profiles are of different devices: /device:TPU:14 before, /device:TPU:15 now
where the time goes in v3:
time: 144 us
  Pallas kernels  141 us (98%)
  local copies, waits for them, and re-layouts  2.34 us (2%)
    pallas_call x1, Pallas kernels, mixer(): pl.pallas_call(functools.partial(mixer_kernel, n, parts), out_shape=jax.S...  141 us

profile of v3, /device:TPU:15, one launch (start us, length us, event | category | flops | bytes accessed | tf_op | source)
XLA Modules:
  0.0 143.7 jit_solution(4782220693518631436)
XLA Ops:
  0.0 141.4 %mixer.1 = bf16[136,4096]{1,0:T(8,128)(2,1)} custom-call(bf16[3,136,4096]{2,1,0:T(8,128)(2,1)} %feat_ref.1, f32[3,3,4096]{2,1,0:T(4,128)} %short_ref.1, f32[128,4096]{1,0:T(8,128)} %long_ref.1, f32[1,4096]{1,0:T(1,128)} %bitcast.1, bf16[4096,512]{1,0:T(8,128)(2,1)} %weight_ref.1), custom_call_target="tpu_custom_call" | custom-call | flops 9663676416 | bytes 8388608 | tf_op jit(solution)/shard_map/mixer/pallas_call | solution.py:425
  141.4 2.3 %copy.7 = bf16[136,4096]{1,0:T(8,128)(2,1)} copy(bf16[136,4096]{1,0:T(8,128)(2,1)} %mixer.1) | data formatting | bytes 2228224

commit v4 on v3

--- a/solution.py
+++ b/solution.py
@@ -90,9 +90,10 @@
 
 def mixer_kernel(
     n, parts, feat_ref, short_ref, long_ref, skip_ref, weight_ref, out_ref,
-    blocks, weights, kept, sent, other, summed, landed, totals, direct, edge_out, edge_in, tail_out, tail_in, ext, prod,
+    blocks, weights, kept, sent, other, summed, landed, relayed, totals, direct, edge_out, edge_in, tail_out, tail_in,
+    ext, prod, before,
     own_sem, edge_sem, tail_send, tail_recv, block_send, block_recv, weight_send, weight_recv,
-    tp_send, tp_recv, out_send, out_recv,
+    tp_send, tp_recv, out_send, out_recv, relay_send, relay_recv,
 ):
     t, cp = lax.axis_index("tp"), lax.axis_index("cp")
     rows = feat_ref.shape[1]
@@ -102,8 +103,6 @@
     depth = n // 2
     place = x * (n - 1 - z) + (1 - x) * z
     forth = 1 - 2 * core
-    half_owner = chip // depth
-    my_piece = (chip % depth) * 2 + t
 
     def cp_at(ring_place):
         r = (ring_place + 2 * n) % n
@@ -119,7 +118,7 @@
     is_first, is_last = cp == 0, cp == 2 * n - 1
 
     barrier = pltpu.get_barrier_semaphore()
-    for device in ((t, ahead), (t, behind), (t, sibling), (1 - t, cp)):
+    for device in ((t, sibling), (1 - t, cp)):
         pl.semaphore_signal(barrier, inc=1, **peer(*device))
 
     @pl.when(cp > 0)
@@ -127,16 +126,11 @@
         pl.semaphore_signal(barrier, inc=1, **peer(t, cp - 1))
 
     def greet(i, carry):
-        sender = (t * depth + i // 2) * 2 + core
-
-        @pl.when(jnp.logical_or(i % 2 != t, sender != cp))
-        def _():
-            pl.semaphore_signal(barrier, inc=1, **peer(i % 2, sender))
-
-        return carry
-
-    lax.fori_loop(0, n, greet, 0)
-    pl.semaphore_wait(barrier, 4 + n - 1 + (half_owner + t) % 2 + (2 * n - 1 - cp + 2 * n - 2) // (2 * n - 1))
+        pl.semaphore_signal(barrier, inc=1, **peer(t, cp_at(place + i)))
+        return carry
+
+    lax.fori_loop(1, n, greet, 0)
+    pl.semaphore_wait(barrier, 2 + n - 1 + (2 * n - 1 - cp + 2 * n - 2) // (2 * n - 1))
 
     columns = pltpu.make_async_remote_copy(
         src_ref=weight_ref, dst_ref=weights.at[core], send_sem=weight_send, recv_sem=weight_recv, **peer(t, sibling)
@@ -218,7 +212,7 @@
 
     prod[pl.ds(0, SUB), :] = jnp.zeros((SUB, LANES), jnp.float32)
 
-    def own_rows(index, carry):
+    def own_strip(index, carry):
         lanes = strip_of(index)
         extend(lanes, (1, 2))
         product = short(1, lanes, 0, rows) * short(2, lanes, 0, rows)
@@ -233,7 +227,8 @@
         direct[:, lanes] = total
         return carry
 
-    lax.fori_loop(0, parts * strips, own_rows, 0)
+    def own_rows(p):
+        lax.fori_loop(p * strips, (p + 1) * strips, own_strip, 0)
 
     def send_own(slot, p, device):
         return pltpu.make_async_remote_copy(
@@ -248,19 +243,23 @@
             recv_sem=block_recv.at[slot + 2, p], **peer(t, odd * ahead + (1 - odd) * behind),
         )
 
-    prod[pl.ds(TAPS, SUB), :] = jnp.zeros((SUB, LANES), jnp.float32)
+    before[pl.ds(TAPS, SUB), :] = jnp.zeros((SUB, LANES), jnp.float32)
 
     def gates(p, carry):
+        @pl.when(p + 1 < parts)
+        def _():
+            own_rows(p + 1)
+
         @pl.when(jnp.logical_not(is_first))
         def _():
             tail_copy(p).wait_recv()
 
         def one(s, carry):
             lanes = strip_of(p * strips + s)
-            prod[pl.ds(0, TAPS), :] = tail_in[p, :, strip_of(s)].astype(jnp.float32)
+            before[pl.ds(0, TAPS), :] = tail_in[p, :, strip_of(s)].astype(jnp.float32)
             total = direct[pl.ds(0, TAPS), lanes]
             for r in range(SUB):
-                shifted = prod[pl.ds(SUB - r, TAPS), :]
+                shifted = before[pl.ds(SUB - r, TAPS), :]
                 for m in range(TAPS // SUB):
                     tap = long_ref[pl.ds(SUB * m + r, 1), lanes]
                     count = SUB * (m + 1)
@@ -281,6 +280,7 @@
         send_own(2, p, behind).start()
         return carry
 
+    own_rows(0)
     lax.fori_loop(0, parts, gates, 0)
 
     own_columns.wait()
@@ -295,9 +295,28 @@
     def out_copy(slot):
         odd, step = slot % 2, (slot + 1) // 2
         return pltpu.make_async_remote_copy(
-            src_ref=summed.at[slot], dst_ref=landed.at[my_piece], send_sem=out_send.at[slot],
-            recv_sem=out_recv.at[my_piece], **peer(half_owner, cp_at(place + (1 - 2 * odd) * forth * step)),
+            src_ref=summed.at[slot], dst_ref=landed.at[chip], send_sem=out_send.at[slot],
+            recv_sem=out_recv.at[chip], **peer(t, cp_at(place + (1 - 2 * odd) * forth * step)),
         )
+
+    def arrived(sender):
+        pltpu.make_async_copy(landed.at[sender], landed.at[sender], out_recv.at[sender]).wait()
+
+    def relay_copy(sender):
+        return pltpu.make_async_remote_copy(
+            src_ref=landed.at[sender], dst_ref=relayed.at[sender % depth], send_sem=relay_send.at[sender % depth],
+            recv_sem=relay_recv.at[sender % depth], **peer(1 - t, cp),
+        )
+
+    def relay(distance):
+        for way in ((1,) if distance in (0, depth) else (1, -1)):
+            sender = cp_at(place + way * distance) // 2
+
+            @pl.when(sender // depth != t)
+            def _():
+                if distance:
+                    arrived(sender)
+                relay_copy(sender).start()
 
     width = weights.shape[2]
     tile = min(256, width)
@@ -326,14 +345,9 @@
     def finish(slot):
         tp_copy(slot).wait_recv()
         total = (kept[slot].astype(jnp.float32) + other[slot].astype(jnp.float32)).astype(jnp.bfloat16)
-        stays = jnp.logical_and(slot == 0, half_owner == t)
-
-        @pl.when(stays)
-        def _():
-            landed[my_piece] = total
-
-        @pl.when(jnp.logical_not(stays))
-        def _():
+        if isinstance(slot, int) and slot == 0:
+            landed[chip] = total
+        else:
             summed[slot] = total
             out_copy(slot).start()
 
@@ -350,7 +364,7 @@
     lax.fori_loop(1, parts, lambda p, carry: (multiply(0, p, False), carry)[1], 0)
     emit(0)
 
-    def pair(i, carry):
+    def pair(i):
         odd, even = 2 * i - 1, 2 * i
 
         def both(p, first):
@@ -361,21 +375,25 @@
         lax.fori_loop(1, parts, lambda p, carry: (both(p, False), carry)[1], 0)
         emit(odd)
         emit(even)
-        finish(odd - 1)
-
-        @pl.when(i > 1)
-        def _():
-            finish(odd - 2)
-
-        return carry
-
-    lax.fori_loop(1, depth, pair, 0)
+
+    pair(1)
+    finish(0)
+    relay(0)
+    for i in range(2, depth):
+        pair(i)
+        finish(2 * i - 2)
+        finish(2 * i - 3)
+        if i > 2:
+            relay(i - 2)
     take(n - 1, 0, True)
     finish(n - 2)
     finish(n - 3)
+    relay(depth - 2)
     lax.fori_loop(1, parts, lambda p, carry: (take(n - 1, p, False), carry)[1], 0)
     emit(n - 1)
     finish(n - 1)
+    relay(depth - 1)
+    relay(depth)
 
     columns.wait_send()
 
@@ -398,19 +416,28 @@
     def drain(slot, carry):
         tp_copy(slot).wait_send()
 
-        @pl.when(jnp.logical_not(jnp.logical_and(slot == 0, half_owner == t)))
+        @pl.when(slot > 0)
         def _():
             out_copy(slot).wait_send()
 
         return carry
 
     lax.fori_loop(0, n, drain, 0)
-    for piece in range(n):
-        @pl.when(jnp.logical_not(jnp.logical_and(piece == my_piece, half_owner == t)))
-        def _():
-            pltpu.make_async_copy(landed.at[piece], landed.at[piece], out_recv.at[piece]).wait()
-
-        out_ref[:, pl.ds(piece * width, width)] = landed[piece, pl.ds(0, rows), :]
+
+    def columns_of(piece):
+        return pl.ds(pl.multiple_of(piece * width, width), width)
+
+    for m in range(depth):
+        sender = t * depth + m
+
+        @pl.when(sender != chip)
+        def _():
+            arrived(sender)
+
+        out_ref[:, columns_of(2 * m + t)] = landed[sender, pl.ds(0, rows), :]
+    for m in range(depth):
+        relay_copy((1 - t) * depth + m).wait()
+        out_ref[:, columns_of(2 * m + 1 - t)] = relayed[m, pl.ds(0, rows), :]
 
 
 def mixer(features, short_filter, long_filter, skip_scale, out_weight, n):
@@ -431,14 +458,16 @@
             pltpu.VMEM((n, parts, padded, part), kind),
             pltpu.VMEM((2, channels, width), kind),
             *[pltpu.VMEM((n, padded, width), kind)] * 5,
+            pltpu.VMEM((n // 2, padded, width), kind),
             pltpu.VMEM((2, 2, padded, width), jnp.float32),
             pltpu.VMEM((rows, channels), jnp.float32),
             *[pltpu.VMEM((2 * SUB, channels), kind)] * 2,
             *[pltpu.VMEM((parts, TAPS, part), kind)] * 2,
             pltpu.VMEM((3, SUB + rows, LANES), jnp.float32),
-            pltpu.VMEM((TAPS + 2 * SUB, LANES), jnp.float32),
+            pltpu.VMEM((SUB + rows, LANES), jnp.float32),
+            pltpu.VMEM((TAPS + SUB, LANES), jnp.float32),
             dma, dma((2,)), dma((parts,)), dma((parts,)), dma((n, parts)), dma((n, parts)), dma, dma,
-            dma((n,)), dma((n,)), dma((n,)), dma((n,)),
+            dma((n,)), dma((n,)), dma((n,)), dma((n,)), dma((n // 2,)), dma((n // 2,)),
         ],
         compiler_params=pltpu.CompilerParams(
             collective_id=0, has_side_effects=True, vmem_limit_bytes=56 * 2**20

time: 144 us -> 149 us (1.035)
  the two profiles are of different devices: /device:TPU:15 before, /device:TPU:5 now
where the time goes in v4:
time: 149 us; the launch traced here: 148 us
  Pallas kernels  146 us (98%)
  local copies, waits for them, and re-layouts  2.34 us (2%)
    pallas_call x1, Pallas kernels, mixer(): pl.pallas_call(functools.partial(mixer_kernel, n, parts), out_shape=jax.S...  146 us

profile of v4, /device:TPU:5, one launch (start us, length us, event | category | flops | bytes accessed | tf_op | source)
XLA Modules:
  0.0 148.3 jit_solution(17719438929752169046)
XLA Ops:
  0.0 145.9 %mixer.1 = bf16[136,4096]{1,0:T(8,128)(2,1)} custom-call(bf16[3,136,4096]{2,1,0:T(8,128)(2,1)} %feat_ref.1, f32[3,3,4096]{2,1,0:T(4,128)} %short_ref.1, f32[128,4096]{1,0:T(8,128)} %long_ref.1, f32[1,4096]{1,0:T(1,128)} %bitcast.1, bf16[4096,512]{1,0:T(8,128)(2,1)} %weight_ref.1), custom_call_target="tpu_custom_call" | custom-call | flops 9663676416 | bytes 8388608 | tf_op jit(solution)/shard_map/mixer/pallas_call | solution.py:452
  145.9 2.3 %copy.7 = bf16[136,4096]{1,0:T(8,128)(2,1)} copy(bf16[136,4096]{1,0:T(8,128)(2,1)} %mixer.1) | data formatting | bytes 2228224

commit v5 on v3

--- a/solution.py
+++ b/solution.py
@@ -90,13 +90,13 @@
 
 def mixer_kernel(
     n, parts, feat_ref, short_ref, long_ref, skip_ref, weight_ref, out_ref,
-    blocks, weights, kept, sent, other, summed, landed, totals, direct, edge_out, edge_in, tail_out, tail_in, ext, prod,
+    blocks, weights, kept, sent, other, summed, landed, totals, direct, edge_out, edge_in, tail_out, tail_in, ext, prod, before,
     own_sem, edge_sem, tail_send, tail_recv, block_send, block_recv, weight_send, weight_recv,
     tp_send, tp_recv, out_send, out_recv,
 ):
     t, cp = lax.axis_index("tp"), lax.axis_index("cp")
     rows = feat_ref.shape[1]
-    padded, part = blocks.shape[2:]
+    part = blocks.shape[3]
     core, chip = cp % 2, cp // 2
     x, z = chip % 2, chip // 2
     depth = n // 2
@@ -116,12 +116,18 @@
 
     ahead, behind = cp_at(place + forth), cp_at(place - forth)
     sibling = cp + 1 - 2 * core
+    across = cp_at(n - 1 - place)
+    takes_seventh, takes_sixth = place % depth == 2 - core, place % depth == 1 + core
     is_first, is_last = cp == 0, cp == 2 * n - 1
 
     barrier = pltpu.get_barrier_semaphore()
     for device in ((t, ahead), (t, behind), (t, sibling), (1 - t, cp)):
         pl.semaphore_signal(barrier, inc=1, **peer(*device))
 
+    @pl.when(jnp.logical_or(takes_seventh, takes_sixth))
+    def _():
+        pl.semaphore_signal(barrier, inc=1, **peer(t, across))
+
     @pl.when(cp > 0)
     def _():
         pl.semaphore_signal(barrier, inc=1, **peer(t, cp - 1))
@@ -136,7 +142,8 @@
         return carry
 
     lax.fori_loop(0, n, greet, 0)
-    pl.semaphore_wait(barrier, 4 + n - 1 + (half_owner + t) % 2 + (2 * n - 1 - cp + 2 * n - 2) // (2 * n - 1))
+    has_chord, has_next = (place % depth + 1) // 2 % 2, (4 * n - 3 - cp) // (2 * n - 1)
+    pl.semaphore_wait(barrier, 4 + n - 1 + (half_owner + t) % 2 + has_chord + has_next)
 
     columns = pltpu.make_async_remote_copy(
         src_ref=weight_ref, dst_ref=weights.at[core], send_sem=weight_send, recv_sem=weight_recv, **peer(t, sibling)
@@ -218,7 +225,7 @@
 
     prod[pl.ds(0, SUB), :] = jnp.zeros((SUB, LANES), jnp.float32)
 
-    def own_rows(index, carry):
+    def own_strip(index, carry):
         lanes = strip_of(index)
         extend(lanes, (1, 2))
         product = short(1, lanes, 0, rows) * short(2, lanes, 0, rows)
@@ -233,7 +240,8 @@
         direct[:, lanes] = total
         return carry
 
-    lax.fori_loop(0, parts * strips, own_rows, 0)
+    def own_rows(p):
+        lax.fori_loop(p * strips, (p + 1) * strips, own_strip, 0)
 
     def send_own(slot, p, device):
         return pltpu.make_async_remote_copy(
@@ -248,19 +256,29 @@
             recv_sem=block_recv.at[slot + 2, p], **peer(t, odd * ahead + (1 - odd) * behind),
         )
 
-    prod[pl.ds(TAPS, SUB), :] = jnp.zeros((SUB, LANES), jnp.float32)
+    def chord(source, slot, p):
+        return pltpu.make_async_remote_copy(
+            src_ref=blocks.at[source, p], dst_ref=blocks.at[slot, p], send_sem=block_send.at[slot, p],
+            recv_sem=block_recv.at[slot, p], **peer(t, across),
+        )
+
+    before[pl.ds(TAPS, SUB), :] = jnp.zeros((SUB, LANES), jnp.float32)
 
     def gates(p, carry):
+        @pl.when(p + 1 < parts)
+        def _():
+            own_rows(p + 1)
+
         @pl.when(jnp.logical_not(is_first))
         def _():
             tail_copy(p).wait_recv()
 
         def one(s, carry):
             lanes = strip_of(p * strips + s)
-            prod[pl.ds(0, TAPS), :] = tail_in[p, :, strip_of(s)].astype(jnp.float32)
+            before[pl.ds(0, TAPS), :] = tail_in[p, :, strip_of(s)].astype(jnp.float32)
             total = direct[pl.ds(0, TAPS), lanes]
             for r in range(SUB):
-                shifted = prod[pl.ds(SUB - r, TAPS), :]
+                shifted = before[pl.ds(SUB - r, TAPS), :]
                 for m in range(TAPS // SUB):
                     tap = long_ref[pl.ds(SUB * m + r, 1), lanes]
                     count = SUB * (m + 1)
@@ -268,12 +286,9 @@
                     total = jnp.concatenate((head, total[count:]), axis=0) if count < TAPS else head
             extend(lanes, (0,))
             gate = short(0, lanes, 0, rows)
-            later = jnp.concatenate(
-                (gate[TAPS:] * direct[pl.ds(TAPS, rows - TAPS), lanes],
-                 jnp.zeros((padded - rows, LANES), jnp.float32)), axis=0,
-            )
+            later = gate[TAPS:] * direct[pl.ds(TAPS, rows - TAPS), lanes]
             blocks[0, p, pl.ds(0, TAPS), strip_of(s)] = (gate[:TAPS] * total).astype(jnp.bfloat16)
-            blocks[0, p, pl.ds(TAPS, padded - TAPS), strip_of(s)] = later.astype(jnp.bfloat16)
+            blocks[0, p, pl.ds(TAPS, rows - TAPS), strip_of(s)] = later.astype(jnp.bfloat16)
             return carry
 
         lax.fori_loop(0, strips, one, 0)
@@ -281,6 +296,7 @@
         send_own(2, p, behind).start()
         return carry
 
+    own_rows(0)
     lax.fori_loop(0, parts, gates, 0)
 
     own_columns.wait()
@@ -340,11 +356,27 @@
     def take(slot, p, first):
         pltpu.make_async_copy(blocks.at[slot, p], blocks.at[slot, p], block_recv.at[slot, p]).wait()
 
-        @pl.when(slot + 2 < n)
+        onward = slot + 2 < n
+        onward = jnp.logical_and(onward, jnp.logical_not(jnp.logical_and(slot == n - 3, takes_sixth)))
+        onward = jnp.logical_and(onward, jnp.logical_not(jnp.logical_and(slot == n - 4, takes_seventh)))
+
+        @pl.when(onward)
         def _():
             pass_on(slot, p).start()
 
+        @pl.when(jnp.logical_and(slot == 2, takes_sixth))
+        def _():
+            chord(2, n - 1, p).start()
+
+        @pl.when(jnp.logical_and(slot == 3, takes_seventh))
+        def _():
+            chord(3, n - 2, p).start()
+
         multiply(slot, p, first)
+
+    def take_last(p, first):
+        pltpu.make_async_copy(blocks.at[n - 1, p], blocks.at[n - 1, p], block_recv.at[n - 1, p]).wait()
+        multiply(n - 1, p, first)
 
     multiply(0, 0, True)
     lax.fori_loop(1, parts, lambda p, carry: (multiply(0, p, False), carry)[1], 0)
@@ -370,10 +402,10 @@
         return carry
 
     lax.fori_loop(1, depth, pair, 0)
-    take(n - 1, 0, True)
+    take_last(0, True)
     finish(n - 2)
     finish(n - 3)
-    lax.fori_loop(1, parts, lambda p, carry: (take(n - 1, p, False), carry)[1], 0)
+    lax.fori_loop(1, parts, lambda p, carry: (take_last(p, False), carry)[1], 0)
     emit(n - 1)
     finish(n - 1)
 
@@ -410,12 +442,11 @@
         def _():
             pltpu.make_async_copy(landed.at[piece], landed.at[piece], out_recv.at[piece]).wait()
 
-        out_ref[:, pl.ds(piece * width, width)] = landed[piece, pl.ds(0, rows), :]
+        out_ref[:, pl.ds(piece * width, width)] = landed[piece]
 
 
 def mixer(features, short_filter, long_filter, skip_scale, out_weight, n):
     _, rows, channels = features.shape
-    padded = -(-rows // 16) * 16
     width = out_weight.shape[1]
     parts = 4
     part = channels // parts
@@ -428,15 +459,16 @@
         in_specs=[whole] * 4 + [pl.BlockSpec(memory_space=pl.ANY)],
         out_specs=whole,
         scratch_shapes=[
-            pltpu.VMEM((n, parts, padded, part), kind),
+            pltpu.VMEM((n, parts, rows, part), kind),
             pltpu.VMEM((2, channels, width), kind),
-            *[pltpu.VMEM((n, padded, width), kind)] * 5,
-            pltpu.VMEM((2, 2, padded, width), jnp.float32),
+            *[pltpu.VMEM((n, rows, width), kind)] * 5,
+            pltpu.VMEM((2, 2, rows, width), jnp.float32),
             pltpu.VMEM((rows, channels), jnp.float32),
             *[pltpu.VMEM((2 * SUB, channels), kind)] * 2,
             *[pltpu.VMEM((parts, TAPS, part), kind)] * 2,
             pltpu.VMEM((3, SUB + rows, LANES), jnp.float32),
-            pltpu.VMEM((TAPS + 2 * SUB, LANES), jnp.float32),
+            pltpu.VMEM((SUB + rows, LANES), jnp.float32),
+            pltpu.VMEM((TAPS + SUB, LANES), jnp.float32),
             dma, dma((2,)), dma((parts,)), dma((parts,)), dma((n, parts)), dma((n, parts)), dma, dma,
             dma((n,)), dma((n,)), dma((n,)), dma((n,)),
         ],
@@ -444,7 +476,7 @@
             collective_id=0, has_side_effects=True, vmem_limit_bytes=56 * 2**20
         ),
         cost_estimate=pl.CostEstimate(
-            flops=4 * n * padded * channels * width, bytes_accessed=4 * channels * width, transcendentals=0
+            flops=4 * n * rows * channels * width, bytes_accessed=4 * channels * width, transcendentals=0
         ),
         name="mixer",
     )(features, short_filter, long_filter, skip_scale.reshape(1, channels), out_weight)

time: 144 us -> 133 us (0.924)
  the two profiles are of different devices: /device:TPU:15 before, /device:TPU:5 now
where the time goes in v5:
time: 133 us
  Pallas kernels  131 us (98%)
  local copies, waits for them, and re-layouts  2.34 us (2%)
    pallas_call x1, Pallas kernels, mixer(): pl.pallas_call(functools.partial(mixer_kernel, n, parts), out_shape=jax.S...  131 us

profile of v5, /device:TPU:5, one launch (start us, length us, event | category | flops | bytes accessed | tf_op | source)
XLA Modules:
  0.0 133.3 jit_solution(17585770543189147666)
XLA Ops:
  0.0 131.0 %mixer.1 = bf16[136,4096]{1,0:T(8,128)(2,1)} custom-call(bf16[3,136,4096]{2,1,0:T(8,128)(2,1)} %feat_ref.1, f32[3,3,4096]{2,1,0:T(4,128)} %short_ref.1, f32[128,4096]{1,0:T(8,128)} %long_ref.1, f32[1,4096]{1,0:T(1,128)} %bitcast.1, bf16[4096,512]{1,0:T(8,128)(2,1)} %weight_ref.1), custom_call_target="tpu_custom_call" | custom-call | flops 9126805504 | bytes 8388608 | tf_op jit(solution)/shard_map/mixer/pallas_call | solution.py:456
  131.0 2.3 %copy.7 = bf16[136,4096]{1,0:T(8,128)(2,1)} copy(bf16[136,4096]{1,0:T(8,128)(2,1)} %mixer.1) | data formatting | bytes 2228224

commit v6 on v5

--- a/solution.py
+++ b/solution.py
@@ -143,7 +143,6 @@
 
     lax.fori_loop(0, n, greet, 0)
     has_chord, has_next = (place % depth + 1) // 2 % 2, (4 * n - 3 - cp) // (2 * n - 1)
-    pl.semaphore_wait(barrier, 4 + n - 1 + (half_owner + t) % 2 + has_chord + has_next)
 
     columns = pltpu.make_async_remote_copy(
         src_ref=weight_ref, dst_ref=weights.at[core], send_sem=weight_send, recv_sem=weight_recv, **peer(t, sibling)
@@ -174,19 +173,13 @@
 
     lax.fori_loop(0, parts * strips, edges, 0)
 
-    @pl.when(jnp.logical_not(is_last))
-    def _():
-        edge_copy.start()
-
-    own_columns.start()
-
     def short(i, lanes, begin, count):
         total = short_ref[i, pl.ds(0, 1), lanes] * ext[i, pl.ds(SUB + begin, count), :]
         for lag in range(1, SHORT):
             total = total + short_ref[i, pl.ds(lag, 1), lanes] * ext[i, pl.ds(SUB + begin - lag, count), :]
         return total
 
-    def tails(p, carry):
+    def tails(p):
         def one(s, carry):
             lanes = strip_of(p * strips + s)
             for i in (1, 2):
@@ -197,13 +190,21 @@
 
         lax.fori_loop(0, strips, one, 0)
 
+    def send_tail(p):
         @pl.when(jnp.logical_not(is_last))
         def _():
             tail_copy(p).start()
 
-        return carry
-
-    lax.fori_loop(0, parts, tails, 0)
+    tails(0)
+    pl.semaphore_wait(barrier, 4 + n - 1 + (half_owner + t) % 2 + has_chord + has_next)
+
+    @pl.when(jnp.logical_not(is_last))
+    def _():
+        edge_copy.start()
+
+    send_tail(0)
+    own_columns.start()
+    lax.fori_loop(1, parts, lambda p, carry: (tails(p), send_tail(p), carry)[2], 0)
     columns.start()
 
     @pl.when(is_first)
@@ -265,9 +266,7 @@
     before[pl.ds(TAPS, SUB), :] = jnp.zeros((SUB, LANES), jnp.float32)
 
     def gates(p, carry):
-        @pl.when(p + 1 < parts)
-        def _():
-            own_rows(p + 1)
+        own_rows(p)
 
         @pl.when(jnp.logical_not(is_first))
         def _():
@@ -296,7 +295,6 @@
         send_own(2, p, behind).start()
         return carry
 
-    own_rows(0)
     lax.fori_loop(0, parts, gates, 0)
 
     own_columns.wait()
@@ -390,15 +388,15 @@
             take(even, p, first)
 
         both(0, True)
+        finish(odd - 1)
+
+        @pl.when(i > 1)
+        def _():
+            finish(odd - 2)
+
         lax.fori_loop(1, parts, lambda p, carry: (both(p, False), carry)[1], 0)
         emit(odd)
         emit(even)
-        finish(odd - 1)
-
-        @pl.when(i > 1)
-        def _():
-            finish(odd - 2)
-
         return carry
 
     lax.fori_loop(1, depth, pair, 0)
@@ -409,6 +407,13 @@
     emit(n - 1)
     finish(n - 1)
 
+    for piece in range(n):
+        @pl.when(jnp.logical_not(jnp.logical_and(piece == my_piece, half_owner == t)))
+        def _():
+            pltpu.make_async_copy(landed.at[piece], landed.at[piece], out_recv.at[piece]).wait()
+
+        out_ref[:, pl.ds(piece * width, width)] = landed[piece]
+
     columns.wait_send()
 
     @pl.when(jnp.logical_not(is_last))
@@ -437,18 +442,12 @@
         return carry
 
     lax.fori_loop(0, n, drain, 0)
-    for piece in range(n):
-        @pl.when(jnp.logical_not(jnp.logical_and(piece == my_piece, half_owner == t)))
-        def _():
-            pltpu.make_async_copy(landed.at[piece], landed.at[piece], out_recv.at[piece]).wait()
-
-        out_ref[:, pl.ds(piece * width, width)] = landed[piece]
 
 
 def mixer(features, short_filter, long_filter, skip_scale, out_weight, n):
     _, rows, channels = features.shape
     width = out_weight.shape[1]
-    parts = 4
+    parts = 8
     part = channels // parts
     kind = jnp.bfloat16
     dma = pltpu.SemaphoreType.DMA

time: 133 us -> 135 us (1.015)
    pallas_call x1, Pallas kernels: 131 us -> 132 us  [mixer(): pl.pallas_call(functools.partial(mixer_kernel, n, parts), out_shape=jax.S...]
where the time goes in v6:
time: 135 us
  Pallas kernels  132 us (98%)
  local copies, waits for them, and re-layouts  2.34 us (2%)
    pallas_call x1, Pallas kernels, mixer(): pl.pallas_call(functools.partial(mixer_kernel, n, parts), out_shape=jax.S...  132 us

profile of v6, /device:TPU:5, one launch (start us, length us, event | category | flops | bytes accessed | tf_op | source)
XLA Modules:
  0.0 134.7 jit_solution(6505524186743619968)
XLA Ops:
  0.0 132.3 %mixer.1 = bf16[136,4096]{1,0:T(8,128)(2,1)} custom-call(bf16[3,136,4096]{2,1,0:T(8,128)(2,1)} %feat_ref.1, f32[3,3,4096]{2,1,0:T(4,128)} %short_ref.1, f32[128,4096]{1,0:T(8,128)} %long_ref.1, f32[1,4096]{1,0:T(1,128)} %bitcast.1, bf16[4096,512]{1,0:T(8,128)(2,1)} %weight_ref.1), custom_call_target="tpu_custom_call" | custom-call | flops 9126805504 | bytes 8388608 | tf_op jit(solution)/shard_map/mixer/pallas_call | solution.py:455
  132.3 2.3 %copy.7 = bf16[136,4096]{1,0:T(8,128)(2,1)} copy(bf16[136,4096]{1,0:T(8,128)(2,1)} %mixer.1) | data formatting | bytes 2228224

commit v7 on v6

--- a/solution.py
+++ b/solution.py
@@ -316,6 +316,9 @@
     width = weights.shape[2]
     tile = min(256, width)
 
+    def bank(slot):
+        return 2 if isinstance(slot, int) and slot == 0 else slot % 2
+
     def multiply(slot, p, first):
         depth_rows = pl.ds(pl.multiple_of(p * part, part), part)
 
@@ -326,16 +329,16 @@
                     blocks[slot, p], weights[side, depth_rows, lanes], preferred_element_type=jnp.float32
                 )
                 if not first:
-                    value = value + totals[slot % 2, side, :, lanes]
-                totals[slot % 2, side, :, lanes] = value
+                    value = value + totals[bank(slot), side, :, lanes]
+                totals[bank(slot), side, :, lanes] = value
             return carry
 
         lax.fori_loop(0, width // tile, one, 0)
 
     def emit(slot):
-        sent[slot] = totals[slot % 2, 1 - t].astype(jnp.bfloat16)
+        sent[slot] = totals[bank(slot), 1 - t].astype(jnp.bfloat16)
         tp_copy(slot).start()
-        kept[slot] = totals[slot % 2, t].astype(jnp.bfloat16)
+        kept[slot] = totals[bank(slot), t].astype(jnp.bfloat16)
 
     def finish(slot):
         tp_copy(slot).wait_recv()
@@ -351,7 +354,7 @@
             summed[slot] = total
             out_copy(slot).start()
 
-    def take(slot, p, first):
+    def receive(slot, p):
         pltpu.make_async_copy(blocks.at[slot, p], blocks.at[slot, p], block_recv.at[slot, p]).wait()
 
         onward = slot + 2 < n
@@ -370,36 +373,39 @@
         def _():
             chord(3, n - 2, p).start()
 
-        multiply(slot, p, first)
-
     def take_last(p, first):
         pltpu.make_async_copy(blocks.at[n - 1, p], blocks.at[n - 1, p], block_recv.at[n - 1, p]).wait()
         multiply(n - 1, p, first)
 
-    multiply(0, 0, True)
-    lax.fori_loop(1, parts, lambda p, carry: (multiply(0, p, False), carry)[1], 0)
-    emit(0)
+    def both(i, p, first):
+        odd, even = 2 * i - 1, 2 * i
+        receive(odd, p)
+        receive(even, p)
+        if isinstance(i, int):
+            multiply(0, p, first)
+        multiply(odd, p, first)
+        multiply(even, p, first)
+
+    both(1, 0, True)
+    lax.fori_loop(1, parts, lambda p, carry: (both(1, p, False), carry)[1], 0)
+    for slot in range(3):
+        emit(slot)
 
     def pair(i, carry):
-        odd, even = 2 * i - 1, 2 * i
-
-        def both(p, first):
-            take(odd, p, first)
-            take(even, p, first)
-
-        both(0, True)
-        finish(odd - 1)
-
-        @pl.when(i > 1)
-        def _():
-            finish(odd - 2)
-
-        lax.fori_loop(1, parts, lambda p, carry: (both(p, False), carry)[1], 0)
-        emit(odd)
-        emit(even)
-        return carry
-
-    lax.fori_loop(1, depth, pair, 0)
+        both(i, 0, True)
+
+        @pl.when(i == 2)
+        def _():
+            finish(0)
+
+        finish(2 * i - 2)
+        finish(2 * i - 3)
+        lax.fori_loop(1, parts, lambda p, carry: (both(i, p, False), carry)[1], 0)
+        emit(2 * i - 1)
+        emit(2 * i)
+        return carry
+
+    lax.fori_loop(2, depth, pair, 0)
     take_last(0, True)
     finish(n - 2)
     finish(n - 3)
@@ -447,7 +453,7 @@
 def mixer(features, short_filter, long_filter, skip_scale, out_weight, n):
     _, rows, channels = features.shape
     width = out_weight.shape[1]
-    parts = 8
+    parts = 4
     part = channels // parts
     kind = jnp.bfloat16
     dma = pltpu.SemaphoreType.DMA
@@ -461,7 +467,7 @@
             pltpu.VMEM((n, parts, rows, part), kind),
             pltpu.VMEM((2, channels, width), kind),
             *[pltpu.VMEM((n, rows, width), kind)] * 5,
-            pltpu.VMEM((2, 2, rows, width), jnp.float32),
+            pltpu.VMEM((3, 2, rows, width), jnp.float32),
             pltpu.VMEM((rows, channels), jnp.float32),
             *[pltpu.VMEM((2 * SUB, channels), kind)] * 2,
             *[pltpu.VMEM((parts, TAPS, part), kind)] * 2,

time: 135 us -> 134 us (level)
  no operation moved by 1% of the time
where the time goes in v7:
time: 134 us; the launch traced here: 133 us
  Pallas kernels  131 us (98%)
  local copies, waits for them, and re-layouts  2.34 us (2%)
    pallas_call x1, Pallas kernels, mixer(): pl.pallas_call(functools.partial(mixer_kernel, n, parts), out_shape=jax.S...  131 us

profile of v7, /device:TPU:5, one launch (start us, length us, event | category | flops | bytes accessed | tf_op | source)
XLA Modules:
  0.0 133.4 jit_solution(2044425913055317436)
XLA Ops:
  0.0 131.0 %mixer.1 = bf16[136,4096]{1,0:T(8,128)(2,1)} custom-call(bf16[3,136,4096]{2,1,0:T(8,128)(2,1)} %feat_ref.1, f32[3,3,4096]{2,1,0:T(4,128)} %short_ref.1, f32[128,4096]{1,0:T(8,128)} %long_ref.1, f32[1,4096]{1,0:T(1,128)} %bitcast.1, bf16[4096,512]{1,0:T(8,128)(2,1)} %weight_ref.1), custom_call_target="tpu_custom_call" | custom-call | flops 9126805504 | bytes 8388608 | tf_op jit(solution)/shard_map/mixer/pallas_call | solution.py:461
  131.0 2.3 %copy.7 = bf16[136,4096]{1,0:T(8,128)(2,1)} copy(bf16[136,4096]{1,0:T(8,128)(2,1)} %mixer.1) | data formatting | bytes 2228224

commit v8 on v6

--- a/solution.py
+++ b/solution.py
@@ -266,7 +266,9 @@
     before[pl.ds(TAPS, SUB), :] = jnp.zeros((SUB, LANES), jnp.float32)
 
     def gates(p, carry):
-        own_rows(p)
+        @pl.when(p + 1 < parts)
+        def _():
+            own_rows(p + 1)
 
         @pl.when(jnp.logical_not(is_first))
         def _():
@@ -295,6 +297,7 @@
         send_own(2, p, behind).start()
         return carry
 
+    own_rows(0)
     lax.fori_loop(0, parts, gates, 0)
 
     own_columns.wait()
@@ -447,7 +450,7 @@
 def mixer(features, short_filter, long_filter, skip_scale, out_weight, n):
     _, rows, channels = features.shape
     width = out_weight.shape[1]
-    parts = 8
+    parts = 4
     part = channels // parts
     kind = jnp.bfloat16
     dma = pltpu.SemaphoreType.DMA

time: 135 us -> 133 us (0.985)
    pallas_call x1, Pallas kernels: 132 us -> 131 us  [mixer(): pl.pallas_call(functools.partial(mixer_kernel, n, parts), out_shape=jax.S...]
where the time goes in v8:
time: 133 us
  Pallas kernels  131 us (98%)
  local copies, waits for them, and re-layouts  2.34 us (2%)
    pallas_call x1, Pallas kernels, mixer(): pl.pallas_call(functools.partial(mixer_kernel, n, parts), out_shape=jax.S...  131 us

profile of v8, /device:TPU:5, one launch (start us, length us, event | category | flops | bytes accessed | tf_op | source)
XLA Modules:
  0.0 133.2 jit_solution(3922983231654720884)
XLA Ops:
  0.0 130.8 %mixer.1 = bf16[136,4096]{1,0:T(8,128)(2,1)} custom-call(bf16[3,136,4096]{2,1,0:T(8,128)(2,1)} %feat_ref.1, f32[3,3,4096]{2,1,0:T(4,128)} %short_ref.1, f32[128,4096]{1,0:T(8,128)} %long_ref.1, f32[1,4096]{1,0:T(1,128)} %bitcast.1, bf16[4096,512]{1,0:T(8,128)(2,1)} %weight_ref.1), custom_call_target="tpu_custom_call" | custom-call | flops 9126805504 | bytes 8388608 | tf_op jit(solution)/shard_map/mixer/pallas_call | solution.py:458
  130.8 2.3 %copy.7 = bf16[136,4096]{1,0:T(8,128)(2,1)} copy(bf16[136,4096]{1,0:T(8,128)(2,1)} %mixer.1) | data formatting | bytes 2228224
